TPU v7x, 32 devices: a whole 2x2x4 slice. The times are simulated.
32 devices in a mesh: shard: 2 (over y), ctx: 4 (over z), tp: 4 (over x, core).
Axes of the slice: x: 2, y: 2, z: 4, core: 2. Of those that a mesh axis runs over, the one named last changes fastest.
Arguments:
- tokens: bfloat16 [2, 2048, 768], P('shard', 'ctx'), may hold values from -6 to 6
- segments: int32 [2, 2048], P('shard', 'ctx'), may hold values from 0 to 8, as said below
- gain_one: bfloat16 [768], P(('shard', 'ctx')), may hold values from 0.5 to 1.5
- shift_one: bfloat16 [768], P(('shard', 'ctx')), may hold values from -4 to 4
- qkv_weight: bfloat16 [768, 12, 192], P(('shard', 'ctx'), 'tp'), may hold values from -0.21875 to 0.21875
- qv_bias: bfloat16 [12, 128], P('tp', ('shard', 'ctx')), may hold values from -3 to 3
- proj_weight: bfloat16 [12, 64, 768], P('tp', None, ('shard', 'ctx')), may hold values from -0.875 to 0.875
- proj_bias: bfloat16 [768], P(('shard', 'ctx')), may hold values from -6 to 6
- gain_two: bfloat16 [768], P(('shard', 'ctx')), may hold values from 0.5 to 1.5
- shift_two: bfloat16 [768], P(('shard', 'ctx')), may hold values from -4 to 4
- up_weight: bfloat16 [768, 3072], P(('shard', 'ctx'), 'tp'), may hold values from -0.21875 to 0.21875
- up_bias: bfloat16 [24, 128], P('tp', ('shard', 'ctx')), may hold values from -6 to 6
- down_weight: bfloat16 [3072, 768], P('tp', ('shard', 'ctx')), may hold values from -0.109375 to 0.109375
- down_bias: bfloat16 [768], P(('shard', 'ctx')), may hold values from -6 to 6
- cotangent: bfloat16 [2, 2048, 768], P('shard', 'ctx'), may hold values from -6 to 6
Outputs:
- layer_out: bfloat16 [2, 2048, 768], P('shard', 'ctx')
- input_grad: float32 [2, 2048, 768], P('shard', 'ctx')
- gain_one_grad: float32 [768], P(('shard', 'ctx'))
- shift_one_grad: float32 [768], P(('shard', 'ctx'))
- qkv_grad: float32 [768, 12, 192], P(('shard', 'ctx'), 'tp')
- qv_bias_grad: float32 [12, 128], P('tp', ('shard', 'ctx'))
- proj_grad: float32 [12, 64, 768], P('tp', None, ('shard', 'ctx'))
- proj_bias_grad: float32 [768], P(('shard', 'ctx'))
- gain_two_grad: float32 [768], P(('shard', 'ctx'))
- shift_two_grad: float32 [768], P(('shard', 'ctx'))
- up_grad: float32 [768, 3072], P(('shard', 'ctx'), 'tp')
- up_bias_grad: float32 [24, 128], P('tp', ('shard', 'ctx'))
- down_grad: float32 [3072, 768], P('tp', ('shard', 'ctx'))
- down_bias_grad: float32 [768], P(('shard', 'ctx'))
Inputs may be any that keep to these rules, and one draw needn't show every extreme that they name: `segments`: document numbers never fall along a sequence; in every sequence one document starts within the first 512 tokens and ends within the last 512.
All inputs are finite; a program needn't handle non-finite values.
Results may differ from a plain program's by a relative error of at most 0.03.
Values may be sent and summed in bfloat16 or wider, within the bound.
A program may use at most 128 MiB of HBM per device.

v0:
```python
import math

import jax
import jax.numpy as jnp
from jax import lax
from jax.sharding import PartitionSpec as P

eps_norm = 1e-05
masked_value = -1e30
gelu_coeff = 0.7978845608028654


def layer_norm(values, gain, shift):
    center = values - jnp.mean(values, axis=-1, keepdims=True)
    spread = jnp.mean(center * center, axis=-1, keepdims=True)
    return center * lax.rsqrt(spread + eps_norm) * gain + shift


def gelu_tanh(values):
    return (
        0.5 * values * (1.0 + jnp.tanh(gelu_coeff * (values + 0.044715 * values * values * values)))
    )


def inner(left, right):
    return lax.dot_general(
        left, right, (((0,), (0,)), ((), ())), preferred_element_type=jnp.float32
    )


def outer(left, right):
    return lax.dot_general(
        left, right, (((1,), (1,)), ((), ())), preferred_element_type=jnp.float32
    )


def block_rows(count):
    return math.gcd(count, 512)


def forward_fold(carry, piece, query_seq, query_seg, query_pos, scale):
    key_piece, value_piece, seg_piece = piece
    count = key_piece.shape[0]
    step_rows = block_rows(count)
    number = count // step_rows
    heads_dev = query_seq.shape[1]
    head_size = query_seq.shape[2]
    key_blocks = key_piece.reshape(number, step_rows, heads_dev, head_size)
    value_blocks = value_piece.reshape(number, step_rows, heads_dev, head_size)
    seg_blocks = seg_piece.reshape(number, step_rows)
    offsets = step_rows * jnp.arange(number, dtype=jnp.int32)

    def forward_visit(state, inputs):
        top, total, accum = state
        key_block, value_block, seg_block, offset = inputs
        key_pos = offset + jnp.arange(step_rows, dtype=jnp.int32)
        allowed = (key_pos[None, :] <= query_pos[:, None]) & (
            seg_block[None, :] == query_seg[:, None]
        )
        scores = (
            jnp.einsum("qhd,khd->hqk", query_seq, key_block, preferred_element_type=jnp.float32)
            * scale
        )
        scores = jnp.where(allowed[None], scores, masked_value)
        new_top = jnp.maximum(top, jnp.max(scores, axis=-1))
        weights = jnp.where(allowed[None], jnp.exp(scores - new_top[:, :, None]), 0.0)
        rescale = jnp.exp(top - new_top)
        total = total * rescale + jnp.sum(weights, axis=-1)
        accum = accum * rescale[:, :, None] + jnp.einsum(
            "hqk,khd->hqd",
            weights.astype(jnp.bfloat16),
            value_block,
            preferred_element_type=jnp.float32,
        )
        return ((new_top, total, accum), None)

    state, unused = lax.scan(forward_visit, carry, (key_blocks, value_blocks, seg_blocks, offsets))
    return state


def back_by_keys(
    carry, piece, query_head, grad_head, lse_head, delta_head, seg_seq, query_pos, scale
):
    pair_piece, seg_piece = piece
    count = pair_piece.shape[0]
    step_rows = block_rows(count)
    number = count // step_rows
    heads_here = query_head.shape[1]
    head_size = query_head.shape[2]
    pair_blocks = pair_piece.reshape(number, step_rows, heads_here, 2 * head_size)
    seg_blocks = seg_piece.reshape(number, step_rows)
    offsets = step_rows * jnp.arange(number, dtype=jnp.int32)

    def back_visit(state, inputs):
        query_acc, pair_acc = state
        pair_block, seg_block, offset = inputs
        key_block = pair_block[:, :, :head_size]
        value_block = pair_block[:, :, head_size:]
        key_pos = offset + jnp.arange(step_rows, dtype=jnp.int32)
        allowed = (key_pos[None, :] <= query_pos[:, None]) & (
            seg_block[None, :] == seg_seq[:, None]
        )
        scores = (
            jnp.einsum("qhd,khd->hqk", query_head, key_block, preferred_element_type=jnp.float32)
            * scale
        )
        probs = jnp.where(allowed[None], jnp.exp(scores - lse_head[:, :, None]), 0.0)
        prob_grad = jnp.einsum(
            "qhd,khd->hqk", grad_head, value_block, preferred_element_type=jnp.float32
        )
        score_low = (probs * (prob_grad - delta_head[:, :, None])).astype(jnp.bfloat16)
        query_acc = (
            query_acc
            + jnp.einsum("hqk,khd->qhd", score_low, key_block, preferred_element_type=jnp.float32)
            * scale
        )
        key_term = (
            jnp.einsum("hqk,qhd->khd", score_low, query_head, preferred_element_type=jnp.float32)
            * scale
        )
        value_term = jnp.einsum(
            "hqk,qhd->khd",
            probs.astype(jnp.bfloat16),
            grad_head,
            preferred_element_type=jnp.float32,
        )
        current = lax.dynamic_slice_in_dim(pair_acc, offset, step_rows, 0)
        pair_acc = lax.dynamic_update_slice_in_dim(
            pair_acc, current + jnp.concatenate([key_term, value_term], axis=2), offset, 0
        )
        return ((query_acc, pair_acc), None)

    state, unused = lax.scan(back_visit, carry, (pair_blocks, seg_blocks, offsets))
    return state


def shards(
    tokens,
    segments,
    gain_one,
    shift_one,
    qkv_weight,
    qv_bias,
    proj_weight,
    proj_bias,
    gain_two,
    shift_two,
    up_weight,
    up_bias,
    down_weight,
    down_bias,
    cotangent,
):
    seq_count, block, width = tokens.shape
    rows = seq_count * block
    (
        gain_first,
        shift_first,
        qkv_full,
        bias_qv,
        proj_full,
        bias_proj,
        gain_second,
        shift_second,
        up_full,
        bias_up,
        down_full,
        bias_down,
    ) = (
        lax.all_gather(gain_one, ("shard", "ctx"), axis=0, tiled=True),
        lax.all_gather(shift_one, ("shard", "ctx"), axis=0, tiled=True),
        lax.all_gather(qkv_weight, ("shard", "ctx"), axis=0, tiled=True),
        lax.all_gather(qv_bias, ("shard", "ctx"), axis=1, tiled=True),
        lax.all_gather(proj_weight, ("shard", "ctx"), axis=2, tiled=True),
        lax.all_gather(proj_bias, ("shard", "ctx"), axis=0, tiled=True),
        lax.all_gather(gain_two, ("shard", "ctx"), axis=0, tiled=True),
        lax.all_gather(shift_two, ("shard", "ctx"), axis=0, tiled=True),
        lax.all_gather(up_weight, ("shard", "ctx"), axis=0, tiled=True),
        lax.all_gather(up_bias, ("shard", "ctx"), axis=1, tiled=True),
        lax.all_gather(down_weight, ("shard", "ctx"), axis=1, tiled=True),
        lax.all_gather(down_bias, ("shard", "ctx"), axis=0, tiled=True),
    )
    heads_dev = qkv_full.shape[1]
    head_size = qkv_full.shape[2] // 3
    scale = head_size ** (-0.5)
    ctx_index = lax.axis_index("ctx")
    seq_total = block * lax.axis_size("ctx")
    local_pos = ctx_index * block + jnp.arange(block, dtype=jnp.int32)
    flat = tokens.reshape(rows, width).astype(jnp.float32)
    norm_first, pull_first = jax.vjp(
        layer_norm, flat, gain_first.astype(jnp.float32), shift_first.astype(jnp.float32)
    )
    input_low = norm_first.astype(jnp.bfloat16)
    projected = jnp.dot(
        input_low,
        qkv_full.reshape(width, heads_dev * 3 * head_size),
        preferred_element_type=jnp.float32,
    ).reshape(rows, heads_dev, 3 * head_size)
    bias_float = bias_qv.astype(jnp.float32)
    query = (projected[:, :, :head_size] + bias_float[:, :head_size]).astype(jnp.bfloat16)
    keys = projected[:, :, head_size : 2 * head_size].astype(jnp.bfloat16)
    values = (projected[:, :, 2 * head_size :] + bias_float[:, head_size:]).astype(jnp.bfloat16)
    member = 0
    query_seq = query
    seg_seq = segments[member]

    def fold_here(carry, piece, start, query_seq=query_seq, seg_seq=seg_seq):
        return forward_fold(carry, piece, query_seq, seg_seq, local_pos, scale)

    start_state = (
        jnp.full((heads_dev, block), masked_value, jnp.float32),
        jnp.zeros((heads_dev, block), jnp.float32),
        jnp.zeros((heads_dev, block, head_size), jnp.float32),
    )
    top, total, accum = fold_here(
        start_state,
        (
            lax.all_gather(keys.reshape(block, heads_dev * head_size), "ctx", axis=0, tiled=True),
            lax.all_gather(values.reshape(block, heads_dev * head_size), "ctx", axis=0, tiled=True),
            lax.all_gather(seg_seq, "ctx", axis=0, tiled=True),
        ),
        jnp.int32(0),
    )
    mixed_parts = jnp.transpose(accum / total[:, :, None], (1, 0, 2))
    stats_parts = jnp.transpose(top + jnp.log(total))
    mixed_low = mixed_parts.reshape(rows, heads_dev * head_size).astype(jnp.bfloat16)
    branch_part = jnp.dot(
        mixed_low,
        proj_full.reshape(heads_dev * head_size, width),
        preferred_element_type=jnp.float32,
    )
    branch = lax.psum(branch_part.astype(jnp.bfloat16), "tp").astype(
        jnp.float32
    ) + bias_proj.astype(jnp.float32)
    resid = flat + branch
    norm_second, pull_second = jax.vjp(
        layer_norm, resid, gain_second.astype(jnp.float32), shift_second.astype(jnp.float32)
    )
    second_low = norm_second.astype(jnp.bfloat16)
    pre_act = jnp.dot(second_low, up_full, preferred_element_type=jnp.float32) + bias_up.astype(
        jnp.float32
    ).reshape(-1)
    active, pull_gelu = jax.vjp(gelu_tanh, pre_act)
    active_low = active.astype(jnp.bfloat16)
    down_part = jnp.dot(active_low, down_full, preferred_element_type=jnp.float32)
    layer_out = (
        resid
        + lax.psum(down_part.astype(jnp.bfloat16), "tp").astype(jnp.float32)
        + bias_down.astype(jnp.float32)
    )
    qkv_back, proj_back, up_back, down_back = (
        lax.all_gather(qkv_weight, ("shard", "ctx"), axis=0, tiled=True),
        lax.all_gather(proj_weight, ("shard", "ctx"), axis=2, tiled=True),
        lax.all_gather(up_weight, ("shard", "ctx"), axis=0, tiled=True),
        lax.all_gather(down_weight, ("shard", "ctx"), axis=1, tiled=True),
    )
    grad_low = cotangent.reshape(rows, width)
    grad_out = grad_low.astype(jnp.float32)
    down_grad = inner(active_low, grad_low)
    down_bias_grad = jnp.sum(grad_out, axis=0)
    act_grad = outer(grad_low, down_back)
    (pre_grad,) = pull_gelu(act_grad)
    pre_low = pre_grad.astype(jnp.bfloat16)
    up_grad = inner(second_low, pre_low)
    up_bias_grad = jnp.sum(pre_low.astype(jnp.float32), axis=0).reshape(bias_up.shape)
    norm_two_grad = lax.psum(outer(pre_low, up_back).astype(jnp.bfloat16), "tp").astype(jnp.float32)
    resid_part, gain_two_grad, shift_two_grad = pull_second(norm_two_grad)
    resid_grad = grad_out + resid_part
    branch_low = resid_grad.astype(jnp.bfloat16)
    proj_bias_grad = jnp.sum(branch_low.astype(jnp.float32), axis=0)
    proj_grad = inner(mixed_low, branch_low).reshape(heads_dev, head_size, width)
    mixed_grad = (
        outer(branch_low, proj_back.reshape(heads_dev * head_size, width))
        .astype(jnp.bfloat16)
        .reshape(rows, heads_dev, head_size)
    )
    delta_all = jnp.sum(mixed_grad.astype(jnp.float32) * mixed_parts, axis=-1)
    groups = [(head, head + 1) for head in range(heads_dev)]
    member = 0
    lower = member * block
    seg_seq = segments[member]
    query_heads = []
    key_heads = []
    value_heads = []
    for first, last in groups:
        count_here = last - first
        query_head = query[lower : lower + block, first:last]
        key_head = keys[lower : lower + block, first:last]
        value_head = values[lower : lower + block, first:last]
        grad_head = mixed_grad[lower : lower + block, first:last]
        lse_rows = stats_parts[lower : lower + block, first:last]
        delta_rows = delta_all[lower : lower + block, first:last]

        def fold_keys(
            carry,
            piece,
            start,
            query_head=query_head,
            grad_head=grad_head,
            lse_head=jnp.transpose(lse_rows),
            delta_head=jnp.transpose(delta_rows),
            seg_seq=seg_seq,
        ):
            return back_by_keys(
                carry, piece, query_head, grad_head, lse_head, delta_head, seg_seq, local_pos, scale
            )

        first_state = (
            jnp.zeros((block, count_here, head_size), jnp.float32),
            jnp.zeros((seq_total, count_here, 2 * head_size), jnp.float32),
        )
        sent_pair = jnp.concatenate([key_head, value_head], axis=2).reshape(
            block, count_here * 2 * head_size
        )
        query_part, pair_total = fold_keys(
            first_state,
            (
                lax.all_gather(sent_pair, "ctx", axis=0, tiled=True),
                lax.all_gather(seg_seq, "ctx", axis=0, tiled=True),
            ),
            jnp.int32(0),
        )
        pair_grad = lax.psum_scatter(
            pair_total.reshape(seq_total, count_here * 2 * head_size).astype(jnp.bfloat16),
            "ctx",
            scatter_dimension=0,
            tiled=True,
        ).astype(jnp.float32)
        pair_grad = pair_grad.reshape(block, count_here, 2 * head_size)
        key_part = pair_grad[:, :, :head_size]
        value_part = pair_grad[:, :, head_size:]
        query_heads.append(query_part)
        key_heads.append(key_part)
        value_heads.append(value_part)
    query_grads = jnp.concatenate(query_heads, axis=1)
    key_grads = jnp.concatenate(key_heads, axis=1)
    value_grads = jnp.concatenate(value_heads, axis=1)
    proj_pieces = jnp.concatenate([query_grads, key_grads, value_grads], axis=2).astype(
        jnp.bfloat16
    )
    proj_low = proj_pieces.reshape(rows, heads_dev * 3 * head_size)
    qkv_grad = inner(input_low, proj_low).reshape(width, heads_dev, 3 * head_size)
    summed_bias = jnp.sum(proj_pieces.astype(jnp.float32), axis=0)
    qv_bias_grad = jnp.concatenate(
        [summed_bias[:, :head_size], summed_bias[:, 2 * head_size :]], axis=1
    )
    norm_one_grad = lax.psum(
        outer(proj_low, qkv_back.reshape(width, heads_dev * 3 * head_size)).astype(jnp.bfloat16),
        "tp",
    ).astype(jnp.float32)
    input_part, gain_one_grad, shift_one_grad = pull_first(norm_one_grad)
    input_grad = resid_grad + input_part
    (
        gain_one_piece,
        shift_one_piece,
        qkv_piece,
        qv_bias_piece,
        proj_piece,
        proj_bias_piece,
        gain_two_piece,
        shift_two_piece,
        up_piece,
        up_bias_piece,
        down_piece,
        down_bias_piece,
    ) = (
        lax.psum_scatter(gain_one_grad, ("shard", "ctx"), scatter_dimension=0, tiled=True),
        lax.psum_scatter(shift_one_grad, ("shard", "ctx"), scatter_dimension=0, tiled=True),
        lax.psum_scatter(qkv_grad, ("shard", "ctx"), scatter_dimension=0, tiled=True),
        lax.psum_scatter(qv_bias_grad, ("shard", "ctx"), scatter_dimension=1, tiled=True),
        lax.psum_scatter(proj_grad, ("shard", "ctx"), scatter_dimension=2, tiled=True),
        lax.psum_scatter(proj_bias_grad, ("shard", "ctx"), scatter_dimension=0, tiled=True),
        lax.psum_scatter(gain_two_grad, ("shard", "ctx"), scatter_dimension=0, tiled=True),
        lax.psum_scatter(shift_two_grad, ("shard", "ctx"), scatter_dimension=0, tiled=True),
        lax.psum_scatter(up_grad, ("shard", "ctx"), scatter_dimension=0, tiled=True),
        lax.psum_scatter(up_bias_grad, ("shard", "ctx"), scatter_dimension=1, tiled=True),
        lax.psum_scatter(down_grad, ("shard", "ctx"), scatter_dimension=1, tiled=True),
        lax.psum_scatter(down_bias_grad, ("shard", "ctx"), scatter_dimension=0, tiled=True),
    )
    return (
        layer_out.astype(jnp.bfloat16).reshape(seq_count, block, width),
        input_grad.reshape(seq_count, block, width),
        gain_one_piece,
        shift_one_piece,
        qkv_piece,
        qv_bias_piece,
        proj_piece,
        proj_bias_piece,
        gain_two_piece,
        shift_two_piece,
        up_piece,
        up_bias_piece,
        down_piece,
        down_bias_piece,
    )


def solution(mesh):
    placed = (
        P("shard", "ctx", None),
        P("shard", "ctx"),
        P(("shard", "ctx")),
        P(("shard", "ctx")),
        P(("shard", "ctx"), "tp", None),
        P("tp", ("shard", "ctx")),
        P("tp", None, ("shard", "ctx")),
        P(("shard", "ctx")),
        P(("shard", "ctx")),
        P(("shard", "ctx")),
        P(("shard", "ctx"), "tp"),
        P("tp", ("shard", "ctx")),
        P("tp", ("shard", "ctx")),
        P(("shard", "ctx")),
        P("shard", "ctx", None),
    )
    return jax.shard_map(
        shards,
        mesh=mesh,
        in_specs=placed,
        out_specs=(
            P("shard", "ctx", None),
            P("shard", "ctx", None),
            P(("shard", "ctx")),
            P(("shard", "ctx")),
            P(("shard", "ctx"), "tp", None),
            P("tp", ("shard", "ctx")),
            P("tp", None, ("shard", "ctx")),
            P(("shard", "ctx")),
            P(("shard", "ctx")),
            P(("shard", "ctx")),
            P(("shard", "ctx"), "tp"),
            P("tp", ("shard", "ctx")),
            P("tp", ("shard", "ctx")),
            P(("shard", "ctx")),
        ),
        check_vma=False,
    )
```

profile of v0, /device:TPU:0, one launch (start us, length us, event | category | flops | bytes accessed | tf_op | source)
XLA Modules:
  0.0 1030.6 jit_solution(7730691538902545156)
XLA Ops:
  15.6 39.1 %all-reduce.13 = (bf16[768]{0:T(1024)(128)(2,1)S(1)}, bf16[768]{0:T(1024)(128)(2,1)S(1)}, bf16[768]{0:T(1024)(128)(2,1)S(1)}, bf16[768]{0:T(1024)(128)(2,1)S(1)}...) all-reduce(bf16[768]{0:T(1024)(128)(2,1)S(1)} %dynamic-update-slice, ...), channel_id=1, replica_groups=mesh['shard'=2,'ctx'=4,'tp'=4] {'shard','ctx'}, use_global_device_ids=true, to_apply=%add.4 | all-reduce | flops 4608 | bytes 18432
  57.6 35.1 %all_gather.64 = bf16[768,3,192]{2,0,1:T(8,128)(2,1)S(1)} all-gather(bf16[96,3,192]{2,0,1:T(8,128)(2,1)S(1)} %copy-done.26), channel_id=1, replica_groups=mesh['shard'=2,'ctx'=4,'tp'=4] {'shard','ctx'}, dimensions={0}, use_global_device_ids=true | all-gather | bytes 995328 | tf_op jit(solution)/shard_map/all_gather | solution.py:172
  93.4 16.9 %all-gather.4 = bf16[8,16,3]{1,2,0:T(4,128)(2,1)S(1)} all-gather(bf16[1,16,3]{1,2,0:T(4,128)(2,1)S(1)} %bitcast.532), channel_id=1, replica_groups=mesh['shard'=2,'ctx'=4,'tp'=4] {'shard','ctx'}, dimensions={0}, use_global_device_ids=true | all-gather | bytes 864 | tf_op jit(solution)/shard_map/all_gather | solution.py:173
  112.9 17.7 %all_gather.67 = bf16[2048,192]{0,1:T(8,128)(2,1)S(1)} all-gather(bf16[512,192]{0,1:T(8,128)(2,1)S(1)} %bitcast.513), channel_id=1, replica_groups=mesh['shard'=2,'ctx'=4,'tp'=4] {'ctx'}, dimensions={0}, use_global_device_ids=true | all-gather | bytes 983040 | tf_op jit(solution)/shard_map/all_gather | solution.py:219
  132.2 15.6 %all_gather.65 = bf16[2048,192]{0,1:T(8,128)(2,1)S(1)} all-gather(bf16[512,192]{0,1:T(8,128)(2,1)S(1)} %bitcast.516), channel_id=1, replica_groups=mesh['shard'=2,'ctx'=4,'tp'=4] {'ctx'}, dimensions={0}, use_global_device_ids=true | all-gather | bytes 983040 | tf_op jit(solution)/shard_map/all_gather | solution.py:218
  162.7 33.6 %while.54 = (s32[]{:T(128)}, f32[3,512]{1,0:T(4,128)S(1)}, f32[3,512]{1,0:T(4,128)S(1)}, f32[3,512,64]{1,2,0:T(8,128)}, s32[4]{0:T(128)}, /*index=5*/s32[4,512]{...) while((s32[]{:T(128)}, f32[3,512]{1,0:T(4,128)S(1)}, ...), condition=%wide.region_5.6_spmd.clone, body=%wide.region_2.5_spmd.clone.sunk | while | flops 212640256 | bytes 15123673 | solution.py:77
  196.4 32.6 %all_gather.68 = bf16[3,64,768]{1,0,2:T(4,128)(2,1)S(1)} all-gather(bf16[3,64,96]{1,0,2:T(4,128)(2,1)S(1)} %copy.80), channel_id=1, replica_groups=mesh['shard'=2,'ctx'=4,'tp'=4] {'shard','ctx'}, dimensions={2}, use_global_device_ids=true | all-gather | bytes 331776 | tf_op jit(solution)/shard_map/all_gather | solution.py:174
  233.1 27.0 %all-gather.5 = bf16[8,16,6]{1,2,0:T(8,128)(2,1)S(1)} all-gather(bf16[1,16,6]{1,2,0:T(8,128)(2,1)S(1)} %bitcast.531), channel_id=1, replica_groups=mesh['shard'=2,'ctx'=4,'tp'=4] {'shard','ctx'}, dimensions={0}, use_global_device_ids=true | all-gather | bytes 1728 | tf_op jit(solution)/shard_map/all_gather | solution.py:179
  260.1 18.7 %all-gather.1 = bf16[2048,1,128]{0,2,1:T(8,128)(2,1)S(1)} all-gather(bf16[512,1,128]{0,2,1:T(8,128)(2,1)S(1)} %pad_maximum_fusion), channel_id=3, replica_groups=mesh['shard'=2,'ctx'=4,'tp'=4] {'ctx'}, dimensions={0}, use_global_device_ids=true | all-gather | bytes 655360 | tf_op jit(solution)/shard_map/all_gather | solution.py:318
  279.9 16.1 %all-gather.2 = bf16[2048,1,128]{0,2,1:T(8,128)(2,1)S(1)} all-gather(bf16[512,1,128]{0,2,1:T(8,128)(2,1)S(1)} %pad_maximum_fusion.1), channel_id=4, replica_groups=mesh['shard'=2,'ctx'=4,'tp'=4] {'ctx'}, dimensions={0}, use_global_device_ids=true | all-gather | bytes 655360 | tf_op jit(solution)/shard_map/all_gather | solution.py:318
  297.0 17.9 %all-gather.3 = bf16[2048,1,128]{0,2,1:T(8,128)(2,1)S(1)} all-gather(bf16[512,1,128]{0,2,1:T(8,128)(2,1)S(1)} %pad_maximum_fusion.2), channel_id=5, replica_groups=mesh['shard'=2,'ctx'=4,'tp'=4] {'ctx'}, dimensions={0}, use_global_device_ids=true | all-gather | bytes 655360 | tf_op jit(solution)/shard_map/all_gather | solution.py:318
  329.8 32.3 %all-reduce.21.cloned.1.call-done = bf16[512,768]{1,0:T(8,128)(2,1)} async-done(((bf16[512,768]{1,0:T(8,128)(2,1)}), bf16[512,768]{1,0:T(8,128)(2,1)}) %all-reduce.21.cloned.1.call-update) | async-done | bytes 786448 | tf_op jit(solution)/shard_map/psum | solution.py:266
  370.6 54.2 %while.55 = (s32[]{:T(128)}, f32[512,1,64]{0,2,1:T(8,128)}, f32[2048,1,128]{0,2,1:T(8,128)}, bf16[4,512,1,128]{3,1,2,0:T(8,128)(2,1)}, s32[4]{0:T(128)}, /*index...) while((s32[]{:T(128)}, f32[512,1,64]{0,2,1:T(8,128)}, ...), condition=%wide.region_15.16_spmd.clone, body=%wide.region_14.15_spmd.clone.sunk | while | flops 170656768 | bytes 7491805 | solution.py:133
  428.1 55.9 %while.56 = (s32[]{:T(128)}, f32[512,1,64]{0,2,1:T(8,128)}, f32[2048,1,128]{0,2,1:T(8,128)}, bf16[4,512,1,128]{3,1,2,0:T(8,128)(2,1)}, s32[4]{0:T(128)}, /*index...) while((s32[]{:T(128)}, f32[512,1,64]{0,2,1:T(8,128)}, ...), condition=%wide.region_17.18_spmd.clone, body=%wide.region_16.17_spmd.clone.sunk | while | flops 170656768 | bytes 7491805 | solution.py:133
  487.4 55.9 %while.57 = (s32[]{:T(128)}, f32[512,1,64]{0,2,1:T(8,128)}, f32[2048,1,128]{0,2,1:T(8,128)}, bf16[4,512,1,128]{3,1,2,0:T(8,128)(2,1)}, s32[4]{0:T(128)}, /*index...) while((s32[]{:T(128)}, f32[512,1,64]{0,2,1:T(8,128)}, ...), condition=%wide.region_19.20_spmd.clone, body=%wide.region_18.19_spmd.clone.sunk | while | flops 170656768 | bytes 7491805 | solution.py:133
  549.5 17.9 %reduce-scatter.20.cloned.1.call-done = bf16[512,128]{0,1:T(8,128)(2,1)} async-done(((bf16[2048,128]{0,1:T(8,128)(2,1)}), bf16[512,128]{0,1:T(8,128)(2,1)}) %reduce-scatter.20.cloned.1.call-update) | async-done | bytes 131088 | tf_op jit(solution)/shard_map/reduce_scatter | solution.py:323
  598.2 32.0 %reduce-scatter.32.cloned.1.call-done = f32[16,6]{1,0:T(8,128)} async-done(((f32[128,6]{1,0:T(8,128)}), f32[16,6]{1,0:T(8,128)}) %reduce-scatter.32.cloned.1.call-update) | async-done | bytes 400
  631.6 62.9 %reduce-scatter.28.cloned.1.call-done = f32[16,3]{1,0:T(8,128)} async-done(((f32[128,3]{1,0:T(8,128)}), f32[16,3]{1,0:T(8,128)}) %reduce-scatter.28.cloned.1.call-update) | async-done | bytes 208
  695.8 63.5 %reduce-scatter.30.cloned.1.call-done = f32[96,192]{1,0:T(8,128)} async-done(((f32[768,192]{1,0:T(8,128)}), f32[96,192]{1,0:T(8,128)}) %reduce-scatter.30.cloned.1.call-update) | async-done | bytes 73744
  761.1 43.4 %all-reduce.23.cloned.1.call-done = (bf16[512,768]{1,0:T(8,128)(2,1)}, bf16[512,768]{1,0:T(8,128)(2,1)}) async-done(((bf16[512,768]{1,0:T(8,128)(2,1)}, bf16[512,768]{1,0:T(8,128)(2,1)}), (bf16[512,768]{1,0:T(8,128)(2,1)}, bf16[512,768]{1,0:T(8,128)(2,1)})) %all-reduce.23.cloned.1.call-update) | async-done | bytes 1572880 | tf_op jit(solution)/shard_map/psum | solution.py:248
  810.0 38.1 %all-reduce.12 = (f32[768]{0:T(1024)S(1)}, f32[768]{0:T(1024)S(1)}, f32[768]{0:T(1024)S(1)}, f32[768]{0:T(1024)S(1)}, f32[768]{0:T(1024)S(1)}, /*index=5*/f32[768]{0:T(1024)S(1)}) all-reduce(f32[768]{0:T(1024)S(1)} %get-tuple-element.662, ...), channel_id=9, replica_groups=mesh['shard'=2,'ctx'=4,'tp'=4] {'shard','ctx'}, use_global_device_ids=true, to_apply=%region_27.28.clone | all-reduce | flops 4608 | bytes 36864
  851.6 26.7 %reduce-scatter.24.cloned.1.call-done = f32[96,768]{1,0:T(8,128)} async-done(((f32[768,768]{1,0:T(8,128)}), f32[96,768]{1,0:T(8,128)}) %reduce-scatter.24.cloned.1.call-update) | async-done | bytes 294928 | tf_op jit(solution)/shard_map/reduce_scatter | solution.py:375
  878.4 72.5 %reduce-scatter.26.cloned.1.call-done = f32[768,96]{0,1:T(8,128)} async-done(((f32[768,768]{0,1:T(8,128)}), f32[768,96]{0,1:T(8,128)}) %reduce-scatter.26.cloned.1.call-update) | async-done | bytes 294928 | tf_op jit(solution)/shard_map/reduce_scatter | solution.py:377
  950.8 72.3 %reduce-scatter.22.cloned.1.call-done = f32[96,3,192]{2,0,1:T(8,128)} async-done(((f32[768,3,192]{2,0,1:T(8,128)}), f32[96,3,192]{2,0,1:T(8,128)}) %reduce-scatter.22.cloned.1.call-update) | async-done | bytes 221200 | tf_op jit(solution)/shard_map/reduce_scatter | solution.py:369
  (451 shorter events, 291.5 us)
Async XLA Ops:
  8.0 49.5 %copy-start.26 = (bf16[96,3,192]{2,0,1:T(8,128)(2,1)S(1)}, bf16[96,3,192]{2,0,1:T(8,128)(2,1)}, u32[]{:S(2)}) copy-start(bf16[96,3,192]{2,0,1:T(8,128)(2,1)} %param.27) | copy-start | bytes 331780
  8.0 308.0 %all-reduce.19.cloned.1.call-start = ((), (), s32[]{:S(2)}) async-start(), calls=%async_computation.9 | async-start | bytes 1572864 | tf_op jit(solution)/shard_map/psum | solution.py:232
  54.7 55.8 %copy-start.31 = (f32[768]{0:T(1024)}, f32[768]{0:T(1024)S(1)}, u32[]{:S(2)}) copy-start(f32[768]{0:T(1024)S(1)} %convert_element_type.165) | copy-start | bytes 9220
  54.7 55.8 %copy-start.50 = (f32[768]{0:T(1024)}, f32[768]{0:T(1024)S(1)}, u32[]{:S(2)}) copy-start(f32[768]{0:T(1024)S(1)} %convert_element_type.166) | copy-start | bytes 9220
  56.0 54.5 %copy-start.33 = (f32[512]{0:T(512)}, f32[512]{0:T(512)S(1)}, u32[]{:S(2)}) copy-start(f32[512]{0:T(512)S(1)} %broadcast_multiply_fusion.1) | copy-start | bytes 6148
  57.6 52.9 %copy-start.40 = (f32[512]{0:T(512)}, f32[512]{0:T(512)S(1)}, u32[]{:S(2)}) copy-start(f32[512]{0:T(512)S(1)} %fusion.119) | copy-start | bytes 6148
  57.6 52.9 %copy-start = (bf16[1,512,768]{2,1,0:T(8,128)(2,1)S(1)}, bf16[1,512,768]{2,1,0:T(8,128)(2,1)}, u32[]{:S(2)}) copy-start(bf16[1,512,768]{2,1,0:T(8,128)(2,1)} %param.23) | copy-start | bytes 2359300
  230.8 87.3 %all-gather.9.cloned.1.call-start = ((), (), s32[]{:S(2)}) async-start(), calls=%async_computation.10 | async-start | bytes 1327104 | tf_op jit(solution)/shard_map/all_gather | solution.py:178
  231.4 90.3 %all-gather.11.cloned.1.call-start = ((), (), s32[]{:S(2)}) async-start(), calls=%async_computation.11 | async-start | bytes 1327104 | tf_op jit(solution)/shard_map/all_gather | solution.py:180
  232.0 130.2 %all-reduce.21.cloned.1.call-start = ((), (), s32[]{:S(2)}) async-start(), calls=%async_computation.12 | async-start | bytes 1572864 | tf_op jit(solution)/shard_map/psum | solution.py:266
  233.0 133.2 %copy-start.24 = (f32[768]{0:T(1024)}, f32[768]{0:T(1024)S(1)}, u32[]{:S(2)}) copy-start(f32[768]{0:T(1024)S(1)} %convert_element_type.175) | copy-start | bytes 9220
  233.0 133.2 %copy-start.27 = (f32[768]{0:T(1024)}, f32[768]{0:T(1024)S(1)}, u32[]{:S(2)}) copy-start(f32[768]{0:T(1024)S(1)} %convert_element_type.176) | copy-start | bytes 9220
  233.1 85.0 %copy-start.52 = (f32[768]{0:T(1024)}, f32[768]{0:T(1024)S(1)}, u32[]{:S(2)}) copy-start(f32[768]{0:T(1024)S(1)} %convert_element_type.177) | copy-start | bytes 9220
  328.5 217.9 %reduce-scatter.16.cloned.1.call-start = ((), (), s32[]{:S(2)}) async-start(), calls=%async_computation.13 | async-start | bytes 655360 | tf_op jit(solution)/shard_map/reduce_scatter | solution.py:323
  426.9 121.0 %reduce-scatter.18.cloned.1.call-start = ((), (), s32[]{:S(2)}) async-start(), calls=%async_computation.14 | async-start | bytes 655360 | tf_op jit(solution)/shard_map/reduce_scatter | solution.py:323
  486.1 81.3 %reduce-scatter.20.cloned.1.call-start = ((), (), s32[]{:S(2)}) async-start(), calls=%async_computation.15 | async-start | bytes 655360 | tf_op jit(solution)/shard_map/reduce_scatter | solution.py:323
  545.5 84.7 %reduce-scatter.32.cloned.1.call-start = ((), (), s32[]{:S(2)}) async-start(), calls=%async_computation.21 | async-start | bytes 73728
  546.3 148.1 %reduce-scatter.28.cloned.1.call-start = ((), (), s32[]{:S(2)}) async-start(), calls=%async_computation.19 | async-start | bytes 73728
  571.0 188.4 %reduce-scatter.30.cloned.1.call-start = ((), (), s32[]{:S(2)}) async-start(), calls=%async_computation.20 | async-start | bytes 884736
  578.3 226.1 %all-reduce.23.cloned.1.call-start = ((), (), s32[]{:S(2)}) async-start(), calls=%async_computation.22 | async-start | bytes 3145728 | tf_op jit(solution)/shard_map/psum | solution.py:248
  584.0 294.3 %reduce-scatter.24.cloned.1.call-start = ((), (), s32[]{:S(2)}) async-start(), calls=%async_computation.17 | async-start | bytes 2654208 | tf_op jit(solution)/shard_map/reduce_scatter | solution.py:375
  587.6 363.3 %reduce-scatter.26.cloned.1.call-start = ((), (), s32[]{:S(2)}) async-start(), calls=%async_computation.18 | async-start | bytes 2654208 | tf_op jit(solution)/shard_map/reduce_scatter | solution.py:377
  592.6 430.6 %reduce-scatter.22.cloned.1.call-start = ((), (), s32[]{:S(2)}) async-start(), calls=%async_computation.16 | async-start | bytes 2654208 | tf_op jit(solution)/shard_map/reduce_scatter | solution.py:369
  596.8 209.4 %copy-start.45 = (f32[512]{0:T(512)S(1)}, f32[512]{0:T(512)}, u32[]{:S(2)}) copy-start(f32[512]{0:T(512)} %copy-done.44) | copy-start | bytes 6148
  (56 other events, 470.7 us)
Sparse Core Ops, SparseCore 0:
  230.9 32.2 all-reduce.18
  328.6 33.4 all-reduce.20
  427.1 21.6 reduce-scatter.15
  486.2 21.6 reduce-scatter.17
  545.6 21.6 reduce-scatter.19
  570.6 59.5 reduce-scatter.31
  634.2 60.2 reduce-scatter.27
  697.8 61.5 reduce-scatter.29
  762.4 41.9 all-reduce.22
  808.8 69.5 reduce-scatter.23
  882.8 67.9 reduce-scatter.25
  955.2 67.9 reduce-scatter.21
Sparse Core Ops, SparseCore 1:
  233.4 42.5 all-gather.8
  277.9 41.2 all-gather.10
where the time goes:
time: 1040 us; the launch traced here: 1030 us
  waiting for transfers between devices  425 us (41%)
  blocking collectives  287 us (28%)
  matrix products  120 us (12%)
  local copies, waits for them, and re-layouts  101 us (10%)
  other arithmetic  56.6 us (5%)
  loops' own time  23 us (2%)
  between operations  17.7 us (2%)
    unnamed x17, waiting for transfers between devices  160 us
    unnamed x2, blocking collectives  77.2 us
    reduce_scatter x1, waiting for transfers between devices, shards(): lax.psum_scatter(down_grad, ('shard', 'ctx'), scatter_dimension=1, tiled=...  72.5 us
    reduce_scatter x1, waiting for transfers between devices, shards(): lax.psum_scatter(qkv_grad, ('shard', 'ctx'), scatter_dimension=0, tiled=T...  72.3 us
    all_gather x3, blocking collectives, shards(): lax.all_gather(sent_pair, 'ctx', axis=0, tiled=True)  52.8 us
    psum x1, waiting for transfers between devices, shards(): lax.psum(down_part.astype(jnp.bfloat16), 'tp').astype(jnp.float32)  43.4 us
    all_gather x1, blocking collectives, shards(): lax.all_gather(qkv_weight, ('shard', 'ctx'), axis=0, tiled=True)  35.1 us
    all_gather x1, blocking collectives, shards(): lax.all_gather(proj_weight, ('shard', 'ctx'), axis=2, tiled=True)  32.6 us
  transfers between devices with their start and end apart: 14, of which 9 were waited for; matrix products, arithmetic and copies ran while one was open for 15% of the time, Pallas kernels for 0%

commit v1 on v0

v1 whole, which is shorter than its diff:
```python
import jax
import jax.numpy as jnp
from jax import lax
from jax.experimental import pallas as pl
from jax.experimental.pallas import tpu as pltpu
from jax.sharding import PartitionSpec as P

eps_norm = 1e-05
masked_value = -1e30
gelu_coeff = 0.7978845608028654
vmem_bytes = 40 * 1024 * 1024


def layer_norm(values, gain, shift):
    center = values - jnp.mean(values, axis=-1, keepdims=True)
    spread = jnp.mean(center * center, axis=-1, keepdims=True)
    return center * lax.rsqrt(spread + eps_norm) * gain + shift


def gelu_tanh(values):
    return (
        0.5 * values * (1.0 + jnp.tanh(gelu_coeff * (values + 0.044715 * values * values * values)))
    )


def inner(left, right):
    return lax.dot_general(
        left, right, (((0,), (0,)), ((), ())), preferred_element_type=jnp.float32
    )


def outer(left, right):
    return lax.dot_general(
        left, right, (((1,), (1,)), ((), ())), preferred_element_type=jnp.float32
    )


def allowed_here(step, mine, block, seg_q_ref, seg_k_ref):
    query_pos = mine * block + lax.broadcasted_iota(jnp.int32, (block, block), 0)
    key_pos = step * block + lax.broadcasted_iota(jnp.int32, (block, block), 1)
    return (key_pos <= query_pos) & (seg_q_ref[:, :1] == seg_k_ref[0])


def forward_kernel(mine_ref, query_ref, pair_ref, seg_q_ref, seg_k_ref, out_ref, lse_ref, top, total, accum):
    step = pl.program_id(1)
    mine = mine_ref[0]
    block = query_ref.shape[0]

    @pl.when(step == 0)
    def _():
        top[...] = jnp.full_like(top, masked_value)
        total[...] = jnp.zeros_like(total)
        accum[...] = jnp.zeros_like(accum)

    @pl.when(step <= mine)
    def _():
        pair = pair_ref[...]
        scores = outer(query_ref[...], pair)
        scores = jnp.where(
            allowed_here(step, mine, block, seg_q_ref, seg_k_ref), scores, masked_value
        )
        old_top = top[...]
        new_top = jnp.maximum(old_top, jnp.max(scores, axis=-1, keepdims=True))
        weights = jnp.exp(scores - new_top)
        rescale = jnp.exp(old_top - new_top)
        total[...] = total[...] * rescale + jnp.sum(weights, axis=-1, keepdims=True)
        accum[...] = accum[...] * rescale + jnp.dot(
            weights.astype(jnp.bfloat16), pair, preferred_element_type=jnp.float32
        )
        top[...] = new_top

    @pl.when(step == pl.num_programs(1) - 1)
    def _():
        out_ref[...] = accum[...] / total[...]
        lse_ref[...] = jnp.broadcast_to(top[...] + jnp.log(total[...]), lse_ref.shape)


def backward_kernel(
    mine_ref, query_ref, grad_ref, mixed_ref, lse_ref, pair_ref, seg_q_ref, seg_k_ref,
    query_grad_ref, pair_grad_ref, accum, delta,
):
    step = pl.program_id(1)
    mine = mine_ref[0]
    block = query_ref.shape[0]

    @pl.when(step == 0)
    def _():
        accum[...] = jnp.zeros_like(accum)
        delta[...] = jnp.sum(
            grad_ref[...].astype(jnp.float32) * mixed_ref[...], axis=-1, keepdims=True
        )

    @pl.when(step <= mine)
    def _():
        pair = pair_ref[...]
        scores = outer(query_ref[...], pair)
        probs = jnp.where(
            allowed_here(step, mine, block, seg_q_ref, seg_k_ref),
            jnp.exp(scores - lse_ref[:, :1]),
            0.0,
        )
        prob_grad = outer(grad_ref[...], pair)
        score_low = (probs * (prob_grad - delta[...])).astype(jnp.bfloat16)
        accum[...] += jnp.dot(score_low, pair, preferred_element_type=jnp.float32)
        pair_grad_ref[...] = (
            inner(score_low, query_ref[...]) + inner(probs.astype(jnp.bfloat16), grad_ref[...])
        ).astype(pair_grad_ref.dtype)

    @pl.when(step > mine)
    def _():
        pair_grad_ref[...] = jnp.zeros_like(pair_grad_ref)

    @pl.when(step == pl.num_programs(1) - 1)
    def _():
        query_grad_ref[...] = accum[...]


def attend(head_size, mine, query_pad, pairs, seg_q, seg_k):
    block = query_pad.shape[0]
    lanes = pairs.shape[1]
    steps = pairs.shape[0] // block
    pair_wide = 2 * head_size
    heads_dev = lanes // pair_wide
    by_head = pl.BlockSpec((block, pair_wide), lambda h, j, m: (0, h))
    return pl.pallas_call(
        forward_kernel,
        grid_spec=pltpu.PrefetchScalarGridSpec(
            num_scalar_prefetch=1,
            grid=(heads_dev, steps),
            in_specs=[
                by_head,
                pl.BlockSpec((block, pair_wide), lambda h, j, m: (jnp.minimum(j, m[0]), h)),
                pl.BlockSpec((block, 128), lambda h, j, m: (0, 0)),
                pl.BlockSpec((1, 1, block), lambda h, j, m: (jnp.minimum(j, m[0]), 0, 0)),
            ],
            out_specs=[by_head, by_head],
            scratch_shapes=[
                pltpu.VMEM((block, 1), jnp.float32),
                pltpu.VMEM((block, 1), jnp.float32),
                pltpu.VMEM((block, pair_wide), jnp.float32),
            ],
        ),
        out_shape=[jax.ShapeDtypeStruct((block, lanes), jnp.float32)] * 2,
        compiler_params=pltpu.CompilerParams(vmem_limit_bytes=vmem_bytes),
        cost_estimate=pl.CostEstimate(
            flops=4 * block * pairs.shape[0] * lanes,
            bytes_accessed=4 * pairs.size,
            transcendentals=block * pairs.shape[0] * heads_dev,
        ),
    )(mine, query_pad, pairs, seg_q, seg_k)


def attend_back(head_size, mine, query_pad, grad_pad, mixed_wide, lse_wide, pairs, seg_q, seg_k):
    block = query_pad.shape[0]
    lanes = pairs.shape[1]
    steps = pairs.shape[0] // block
    pair_wide = 2 * head_size
    heads_dev = lanes // pair_wide
    by_head = pl.BlockSpec((block, pair_wide), lambda h, j, m: (0, h))
    return pl.pallas_call(
        backward_kernel,
        grid_spec=pltpu.PrefetchScalarGridSpec(
            num_scalar_prefetch=1,
            grid=(heads_dev, steps),
            in_specs=[
                by_head,
                by_head,
                by_head,
                by_head,
                pl.BlockSpec((block, pair_wide), lambda h, j, m: (jnp.minimum(j, m[0]), h)),
                pl.BlockSpec((block, 128), lambda h, j, m: (0, 0)),
                pl.BlockSpec((1, 1, block), lambda h, j, m: (jnp.minimum(j, m[0]), 0, 0)),
            ],
            out_specs=[by_head, pl.BlockSpec((block, pair_wide), lambda h, j, m: (j, h))],
            scratch_shapes=[
                pltpu.VMEM((block, pair_wide), jnp.float32),
                pltpu.VMEM((block, 1), jnp.float32),
            ],
        ),
        out_shape=[
            jax.ShapeDtypeStruct((block, lanes), jnp.float32),
            jax.ShapeDtypeStruct(pairs.shape, jnp.bfloat16),
        ],
        compiler_params=pltpu.CompilerParams(vmem_limit_bytes=vmem_bytes),
        cost_estimate=pl.CostEstimate(
            flops=10 * block * pairs.shape[0] * lanes,
            bytes_accessed=6 * pairs.size,
            transcendentals=block * pairs.shape[0] * heads_dev,
        ),
    )(mine, query_pad, grad_pad, mixed_wide, lse_wide, pairs, seg_q, seg_k)


def columns_of(vector, rows):
    count = -(-vector.shape[-1] // rows)
    padded = jnp.pad(vector, [(0, 0)] * (vector.ndim - 1) + [(0, count * rows - vector.shape[-1])])
    return padded.reshape(vector.shape[:-1] + (count, rows))


def pad_lanes(array):
    extra = -array.shape[-1] % 128
    return jnp.pad(array, [(0, 0)] * (array.ndim - 1) + [(0, extra)])


def gather_owned(array):
    return lax.all_gather(array, ("shard", "ctx"), axis=0, tiled=True)


def scatter_owned(array):
    return lax.psum_scatter(array, ("shard", "ctx"), scatter_dimension=0, tiled=True)


def sum_tp(array):
    return lax.psum(array, "tp")


def shards(
    tokens,
    segments,
    gain_one,
    shift_one,
    qkv_weight,
    qv_bias,
    proj_weight,
    proj_bias,
    gain_two,
    shift_two,
    up_weight,
    up_bias,
    down_weight,
    down_bias,
    cotangent,
):
    seq_count, block, width = tokens.shape
    rows = seq_count * block
    own = qkv_weight.shape[0]
    owners = width // own
    heads_dev = qkv_weight.shape[1]
    head_size = qkv_weight.shape[2] // 3
    hidden = up_weight.shape[1]
    mixed_wide = heads_dev * head_size
    scale = head_size ** (-0.5)
    ctx_size = lax.axis_size("ctx")
    ctx_index = lax.axis_index("ctx")
    shard_index = lax.axis_index("shard")
    low = jnp.bfloat16

    small = jnp.concatenate(
        [
            jnp.stack([gain_one, shift_one, proj_bias, gain_two, shift_two, down_bias]),
            columns_of(jnp.concatenate([qv_bias.reshape(-1), up_bias.reshape(-1)]), own),
            columns_of(segments.reshape(-1).astype(low), own),
        ],
        axis=0,
    )
    packed = jnp.concatenate(
        [
            up_weight,
            down_weight.T,
            qkv_weight.reshape(own, -1),
            proj_weight.reshape(mixed_wide, own).T,
            pad_lanes(small.T),
        ],
        axis=1,
    )
    whole = gather_owned(packed)
    at = 0
    up_full = whole[:, at : at + hidden]
    at += hidden
    down_full = whole[:, at : at + hidden]
    at += hidden
    qkv_full = whole[:, at : at + 3 * mixed_wide]
    at += 3 * mixed_wide
    proj_full = whole[:, at : at + mixed_wide]
    at += mixed_wide
    vectors = whole[:, at:].astype(jnp.float32).T
    gain_first, shift_first, bias_proj, gain_second, shift_second, bias_down = (
        vectors[i] for i in range(6)
    )
    by_owner = vectors.reshape(-1, owners, own)
    bias_each = qv_bias.size + up_bias.size
    bias_rows = -(-bias_each // own)
    bias_flat = (
        by_owner[6 : 6 + bias_rows].transpose(1, 0, 2).reshape(owners, -1)[:, :bias_each]
    )
    bias_qv = (
        bias_flat[:, : qv_bias.size]
        .reshape(owners, heads_dev, -1)
        .transpose(1, 0, 2)
        .reshape(heads_dev, 2 * head_size)
    )
    bias_up = (
        bias_flat[:, qv_bias.size :]
        .reshape(owners, up_bias.shape[0], -1)
        .transpose(1, 0, 2)
        .reshape(-1)
    )
    seg_rows = -(-rows // own)
    seg_all = (
        by_owner[6 + bias_rows : 6 + bias_rows + seg_rows]
        .transpose(1, 0, 2)
        .reshape(owners, -1)[:, :rows]
        .astype(jnp.int32)
    )
    seg_k = lax.dynamic_slice_in_dim(seg_all, shard_index * ctx_size, ctx_size, 0).reshape(
        ctx_size, 1, block
    )
    seg_q = jnp.broadcast_to(segments.reshape(block, 1), (block, 128))
    mine = ctx_index.astype(jnp.int32).reshape(1)

    flat = tokens.reshape(rows, width).astype(jnp.float32)
    norm_first, pull_first = jax.vjp(layer_norm, flat, gain_first, shift_first)
    input_low = norm_first.astype(low)
    projected = jnp.dot(input_low, qkv_full, preferred_element_type=jnp.float32).reshape(
        rows, heads_dev, 3 * head_size
    )
    keys_bias = jnp.concatenate(
        [jnp.zeros((heads_dev, head_size), jnp.float32), bias_qv[:, head_size:]], axis=1
    )
    pair_own = (projected[:, :, head_size:] + keys_bias).astype(low)
    query = (projected[:, :, :head_size] + bias_qv[:, :head_size]).astype(low)
    zero_half = jnp.zeros((rows, heads_dev, head_size), low)
    query_pad = jnp.concatenate([query * low(scale), zero_half], axis=2).reshape(
        rows, 2 * mixed_wide
    )
    pairs = lax.all_gather(pair_own.reshape(rows, 2 * mixed_wide), "ctx", axis=0, tiled=True)
    mixed_pad, lse_wide = attend(head_size, mine, query_pad, pairs, seg_q, seg_k)
    mixed_low = (
        mixed_pad.reshape(rows, heads_dev, 2 * head_size)[:, :, head_size:]
        .reshape(rows, mixed_wide)
        .astype(low)
    )
    branch = sum_tp(outer(mixed_low, proj_full).astype(low)).astype(jnp.float32) + bias_proj
    resid = flat + branch
    norm_second, pull_second = jax.vjp(layer_norm, resid, gain_second, shift_second)
    second_low = norm_second.astype(low)
    pre_act = jnp.dot(second_low, up_full, preferred_element_type=jnp.float32) + bias_up
    active, pull_gelu = jax.vjp(gelu_tanh, pre_act)
    active_low = active.astype(low)
    grad_low = cotangent.reshape(rows, width)
    grad_out = grad_low.astype(jnp.float32)
    act_grad = jnp.dot(grad_low, down_full, preferred_element_type=jnp.float32)
    (pre_grad,) = pull_gelu(act_grad)
    pre_low = pre_grad.astype(low)
    norm_two_grad = sum_tp(outer(pre_low, up_full).astype(low)).astype(jnp.float32)
    layer_out = (
        resid + sum_tp(outer(active_low, down_full).astype(low)).astype(jnp.float32) + bias_down
    )
    resid_part, gain_two_grad, shift_two_grad = pull_second(norm_two_grad)
    resid_grad = grad_out + resid_part
    branch_low = resid_grad.astype(low)
    mixed_grad = (
        jnp.dot(branch_low, proj_full, preferred_element_type=jnp.float32)
        .astype(low)
        .reshape(rows, heads_dev, head_size)
    )
    grad_pad = jnp.concatenate([zero_half, mixed_grad], axis=2).reshape(rows, 2 * mixed_wide)

    up_bias_grad = jnp.sum(pre_low.astype(jnp.float32), axis=0).reshape(up_bias.shape[0], -1)
    up_bias_split = columns_of(
        up_bias_grad.reshape(up_bias.shape[0], owners, -1).transpose(1, 0, 2).reshape(owners, -1),
        own,
    )
    second_small = jnp.concatenate(
        [
            jnp.stack(
                [
                    jnp.sum(grad_out, axis=0),
                    jnp.sum(branch_low.astype(jnp.float32), axis=0),
                    gain_two_grad,
                    shift_two_grad,
                ]
            ),
            up_bias_split.transpose(1, 0, 2).reshape(-1, width),
        ],
        axis=0,
    )
    second_piece = scatter_owned(
        pad_lanes(
            jnp.concatenate(
                [
                    inner(second_low, pre_low).astype(low),
                    inner(grad_low, active_low).astype(low),
                    inner(branch_low, mixed_low).astype(low),
                    second_small.T.astype(low),
                ],
                axis=1,
            )
        )
    ).astype(jnp.float32)

    query_grad, pair_total = attend_back(
        head_size, mine, query_pad, grad_pad, mixed_pad, lse_wide, pairs, seg_q, seg_k
    )
    pair_grad = lax.psum_scatter(pair_total, "ctx", scatter_dimension=0, tiled=True)
    query_part = (query_grad.reshape(rows, heads_dev, 2 * head_size)[:, :, :head_size] * scale).astype(
        low
    )
    proj_low = jnp.concatenate(
        [query_part, pair_grad.reshape(rows, heads_dev, 2 * head_size)], axis=2
    ).reshape(rows, 3 * mixed_wide)
    summed_bias = jnp.sum(proj_low.astype(jnp.float32), axis=0).reshape(heads_dev, 3 * head_size)
    qv_bias_grad = jnp.concatenate(
        [summed_bias[:, :head_size], summed_bias[:, 2 * head_size :]], axis=1
    )
    norm_one_grad = sum_tp(outer(proj_low, qkv_full).astype(low)).astype(jnp.float32)
    input_part, gain_one_grad, shift_one_grad = pull_first(norm_one_grad)
    input_grad = resid_grad + input_part
    qv_split = columns_of(
        qv_bias_grad.reshape(heads_dev, owners, -1).transpose(1, 0, 2).reshape(owners, -1), own
    )
    first_small = jnp.concatenate(
        [jnp.stack([gain_one_grad, shift_one_grad]), qv_split.transpose(1, 0, 2).reshape(-1, width)],
        axis=0,
    )
    first_piece = scatter_owned(
        pad_lanes(
            jnp.concatenate(
                [inner(input_low, proj_low).astype(low), first_small.T.astype(low)], axis=1
            )
        )
    ).astype(jnp.float32)

    up_piece = second_piece[:, :hidden]
    down_piece = second_piece[:, hidden : 2 * hidden].T
    at = 2 * hidden
    proj_piece = second_piece[:, at : at + mixed_wide].T.reshape(heads_dev, head_size, own)
    at += mixed_wide
    second_vectors = second_piece[:, at:].T
    up_bias_piece = second_vectors[4 : 4 + up_bias_split.shape[1]].reshape(-1)[
        : up_bias.size
    ].reshape(up_bias.shape)
    qkv_piece = first_piece[:, : 3 * mixed_wide].reshape(own, heads_dev, 3 * head_size)
    first_vectors = first_piece[:, 3 * mixed_wide :].T
    qv_bias_piece = first_vectors[2 : 2 + qv_split.shape[1]].reshape(-1)[: qv_bias.size].reshape(
        qv_bias.shape
    )
    return (
        layer_out.astype(low).reshape(seq_count, block, width),
        input_grad.reshape(seq_count, block, width),
        first_vectors[0],
        first_vectors[1],
        qkv_piece,
        qv_bias_piece,
        proj_piece,
        second_vectors[1],
        second_vectors[2],
        second_vectors[3],
        up_piece,
        up_bias_piece,
        down_piece,
        second_vectors[0],
    )


def solution(mesh):
    placed = (
        P("shard", "ctx", None),
        P("shard", "ctx"),
        P(("shard", "ctx")),
        P(("shard", "ctx")),
        P(("shard", "ctx"), "tp", None),
        P("tp", ("shard", "ctx")),
        P("tp", None, ("shard", "ctx")),
        P(("shard", "ctx")),
        P(("shard", "ctx")),
        P(("shard", "ctx")),
        P(("shard", "ctx"), "tp"),
        P("tp", ("shard", "ctx")),
        P("tp", ("shard", "ctx")),
        P(("shard", "ctx")),
        P("shard", "ctx", None),
    )
    return jax.shard_map(
        shards,
        mesh=mesh,
        in_specs=placed,
        out_specs=(
            P("shard", "ctx", None),
            P("shard", "ctx", None),
            P(("shard", "ctx")),
            P(("shard", "ctx")),
            P(("shard", "ctx"), "tp", None),
            P("tp", ("shard", "ctx")),
            P("tp", None, ("shard", "ctx")),
            P(("shard", "ctx")),
            P(("shard", "ctx")),
            P(("shard", "ctx")),
            P(("shard", "ctx"), "tp"),
            P("tp", ("shard", "ctx")),
            P("tp", ("shard", "ctx")),
            P(("shard", "ctx")),
        ),
        check_vma=False,
    )
```

time: 1040 us -> 489 us (0.47)
  blocking collectives: 287 us -> 0 us
  matrix products: 120 us -> 25.3 us
  waiting for transfers between devices: 425 us -> 367 us
  local copies, waits for them, and re-layouts: 101 us -> 43.8 us
  other arithmetic: 56.6 us -> 22.2 us
  loops' own time: 23 us -> 0 us
  Pallas kernels: 0 us -> 14.1 us
    all_gather x10 -> x0, blocking collectives: 210 us -> none  [the longest x3 52.8 us: shards(): lax.all_gather(sent_pair, 'ctx', axis=0, tiled=True)]
    reduce_scatter x6 -> x1, waiting for transfers between devices: 189 us -> 37.1 us  [shards(): lax.psum_scatter(pair_total, 'ctx', scatter_dimension=0, tiled=True)]
    all_gather x2, waiting for transfers between devices: 0.03 us -> 104 us  [the longest x1 69.9 us: gather_owned(): return lax.all_gather(array, ('shard', 'ctx'), axis=0, tiled=True)]
    dot_general x72 -> x4, matrix products: 99.4 us -> 7.08 us  [the longest x1 2.5 us: shards(): jnp.dot(second_low, up_full, preferred_element_type=jnp.float32) + bias_up]
    unnamed x2 -> x0, blocking collectives: 77.2 us -> none
    unnamed x17 -> x10, waiting for transfers between devices: 160 us -> 123 us
    psum x3, waiting for transfers between devices: 75.7 us -> 103 us  [sum_tp(): return lax.psum(array, 'tp')]
    add x33 -> x0, other arithmetic: 23.3 us -> none  [the longest x12 13.3 us: back_visit(): current + jnp.concatenate([key_term, value_term], axis=2)]
  transfers between devices with their start and end apart: 14 -> 8, of which waited for: 9 -> 8; matrix products, arithmetic and copies ran while one was open for 15% -> 9% of each run, Pallas kernels for 0% -> 0%
where the time goes in v1:
time: 489 us; the launch traced here: 488 us
  waiting for transfers between devices  367 us (75%)
  local copies, waits for them, and re-layouts  43.8 us (9%)
  matrix products  25.3 us (5%)
  other arithmetic  22.2 us (5%)
  between operations  14.8 us (3%)
  Pallas kernels  14.1 us (3%)
    unnamed x10, waiting for transfers between devices  123 us
    psum x3, waiting for transfers between devices, sum_tp(): return lax.psum(array, 'tp')  103 us
    all_gather x1, waiting for transfers between devices, gather_owned(): return lax.all_gather(array, ('shard', 'ctx'), axis=0, tiled=True)  69.9 us
    reduce_scatter x1, waiting for transfers between devices, shards(): lax.psum_scatter(pair_total, 'ctx', scatter_dimension=0, tiled=True)  37.1 us
    all_gather x1, waiting for transfers between devices, shards(): lax.all_gather(pair_own.reshape(rows, 2 * mixed_wide), 'ctx', axis=0, til...  33.8 us
    unnamed x65, local copies, waits for them, and re-layouts  19.5 us
    dot_general x4, matrix products, outer(): lax.dot_general(left, right, (((1,), (1,)), ((), ())), preferred_element_...  10.6 us
  transfers between devices with their start and end apart: 8, of which 8 were waited for; matrix products, arithmetic and copies ran while one was open for 9% of the time, Pallas kernels for 0%

profile of v1, /device:TPU:0, one launch (start us, length us, event | category | flops | bytes accessed | tf_op | source)
XLA Modules:
  0.0 487.9 jit_solution(9994787692997386777)
XLA Ops:
  12.8 1.9 concatenate.41
  15.3 69.9 %all-gather.3.cloned.1.call-done = bf16[768,2432]{1,0:T(8,128)(2,1)} async-done(((bf16[96,2432]{1,0:T(8,128)(2,1)}), bf16[768,2432]{1,0:T(8,128)(2,1)}) %all-gather.3.cloned.1.call-update) | async-done | bytes 3735568 | tf_op jit(solution)/shard_map/all_gather | solution.py:205
  94.8 33.8 %all-gather.5.cloned.1.call-done.pair_ref = bf16[2048,384]{1,0:T(8,128)(2,1)} async-done(((bf16[512,384]{1,0:T(8,128)(2,1)}), bf16[2048,384]{1,0:T(8,128)(2,1)}) %all-gather.5.cloned.1.call-update) | async-done | bytes 1572880 | tf_op jit(solution)/shard_map/all_gather | solution.py:325
  130.2 5.4 %shard_map.254 = (f32[512,384]{1,0:T(8,128)S(1)}, f32[512,384]{1,0:T(8,128)S(1)}) custom-call(s32[1]{0:T(128)} %bitcast.1.mine_ref, bf16[512,384]{1,0:T(8,128)(2,1)S(1)} %copy.95.query_ref, bf16[2048,384]{1,0:T(8,128)(2,1)S(1)} %copy-done, s32[512,128]{1,0:T(8,128)S(1)} %broadcast_in_dim.10.seg_q_ref, s32[4,1,512]{2,1,0:T(1,128)S(1)} %reshape.279.seg_k_ref), custom_call_target="tpu_custom_call" | custom-call | flops 1610612736 | bytes 3145728 | tf_op jit(solution)/shard_map/pallas_call | solution.py:125
  137.5 2.6 convolution_convert_fusion.6
  140.4 45.0 %all-reduce.14.cloned.1.call-done = bf16[512,768]{1,0:T(8,128)(2,1)} async-done(((bf16[512,768]{1,0:T(8,128)(2,1)}), bf16[512,768]{1,0:T(8,128)(2,1)}) %all-reduce.14.cloned.1.call-update) | async-done | bytes 786448 | tf_op jit(solution)/shard_map/psum | solution.py:213
  187.4 2.5 convolution_add_fusion
  194.8 34.6 %all-reduce.16.cloned.1.call-done = bf16[512,768]{1,0:T(8,128)(2,1)} async-done(((bf16[512,768]{1,0:T(8,128)(2,1)}), bf16[512,768]{1,0:T(8,128)(2,1)}) %all-reduce.16.cloned.1.call-update) | async-done | bytes 786448 | tf_op jit(solution)/shard_map/psum | solution.py:213
  229.4 2.1 fusion.9
  233.6 1.9 convolution_convert_fusion.8
  237.2 8.7 %shard_map.255 = (f32[512,384]{1,0:T(8,128)S(1)}, bf16[2048,384]{1,0:T(8,128)(2,1)}) custom-call(s32[1]{0:T(128)} %bitcast.1.mine_ref, bf16[512,384]{1,0:T(8,128)(2,1)S(1)} %copy.95.query_ref, bf16[512,384]{1,0:T(8,128)(2,1)S(1)} %copy.99.grad_ref, f32[512,384]{1,0:T(8,128)S(1)} %get-tuple-element.18.mixed_ref, f32[512,384]{1,0:T(8,128)S(1)} %get-tuple-element.19.lse_ref, ...), custom_call_target="tpu_custom_call" | custom-call | flops 4026531840 | bytes 4718592 | tf_op jit(solution)/shard_map/pallas_call | solution.py:160
  247.7 2.1 convolution_convert_fusion.1
  249.9 3.2 convolution_convert_fusion.4
  253.4 37.1 %reduce-scatter.8.cloned.1.call-done = bf16[512,384]{1,0:T(8,128)(2,1)} async-done(((bf16[2048,384]{1,0:T(8,128)(2,1)}), bf16[512,384]{1,0:T(8,128)(2,1)}) %reduce-scatter.8.cloned.1.call-update) | async-done | bytes 393232 | tf_op jit(solution)/shard_map/reduce_scatter | solution.py:394
  292.7 3.1 convolution_convert_fusion.5
  295.9 3.5 fusion.27
  300.9 2.8 pad_maximum_fusion
  303.8 4.6 copy.113
  308.4 3.6 pad.33.clone
  314.8 23.2 %all-reduce.18.cloned.1.call-done = (bf16[512,768]{1,0:T(8,128)(2,1)}, bf16[512,768]{1,0:T(8,128)(2,1)}) async-done(((bf16[512,768]{1,0:T(8,128)(2,1)}, bf16[512,768]{1,0:T(8,128)(2,1)}), (bf16[512,768]{1,0:T(8,128)(2,1)}, bf16[512,768]{1,0:T(8,128)(2,1)})) %all-reduce.18.cloned.1.call-update) | async-done | bytes 1572880 | tf_op jit(solution)/shard_map/psum | solution.py:213
  343.5 2.3 pad.32.clone
  345.9 3.7 add_bitcast_fusion
  349.6 62.5 %reduce-scatter.12.cloned.1.call-done = bf16[96,1792]{1,0:T(8,128)(2,1)} async-done(((bf16[768,1792]{1,0:T(8,128)(2,1)}), bf16[96,1792]{1,0:T(8,128)(2,1)}) %reduce-scatter.12.cloned.1.call-update) | async-done | bytes 344080
  417.1 60.7 %reduce-scatter.10.cloned.1.call-done = bf16[96,640]{1,0:T(8,128)(2,1)} async-done(((bf16[768,640]{1,0:T(8,128)(2,1)}), bf16[96,640]{1,0:T(8,128)(2,1)}) %reduce-scatter.10.cloned.1.call-update) | async-done | bytes 122896
  (184 shorter events, 52.3 us)
Async XLA Ops:
  7.2 7.6 %copy-start.2 = (bf16[1,512,768]{2,1,0:T(8,128)(2,1)S(1)}, bf16[1,512,768]{2,1,0:T(8,128)(2,1)}, u32[]{:S(2)}) copy-start(bf16[1,512,768]{2,1,0:T(8,128)(2,1)} %param.15) | copy-start | bytes 2359300
  7.2 78.0 %all-gather.3.cloned.1.call-start = ((), (), s32[]{:S(2)}) async-start(), calls=%async_computation.3 | async-start | bytes 4202496 | tf_op jit(solution)/shard_map/all_gather | solution.py:205
  14.7 113.9 %all-gather.5.cloned.1.call-start = ((), (), s32[]{:S(2)}) async-start(), calls=%async_computation.4 | async-start | bytes 1966080 | tf_op jit(solution)/shard_map/all_gather | solution.py:325
  93.0 92.4 %all-reduce.14.cloned.1.call-start = ((), (), s32[]{:S(2)}) async-start(), calls=%async_computation.5 | async-start | bytes 1572864 | tf_op jit(solution)/shard_map/psum | solution.py:213
  93.0 35.6 %copy-start.23 = (s32[1,512]{1,0:T(1,128)S(1)}, s32[1,512]{1,0:T(1,128)}, u32[]{:S(2)}) copy-start(s32[1,512]{1,0:T(1,128)} %param.16) | copy-start | bytes 6148
  137.5 49.4 %copy-start.15 = (bf16[512,3,64]{0,2,1:T(8,128)(2,1)}, bf16[512,3,64]{0,2,1:T(8,128)(2,1)S(1)}, u32[]{:S(2)}) copy-start(bf16[512,3,64]{0,2,1:T(8,128)(2,1)S(1)} %slice.179) | copy-start | bytes 589828
  140.1 89.2 %all-reduce.16.cloned.1.call-start = ((), (), s32[]{:S(2)}) async-start(), calls=%async_computation.6 | async-start | bytes 1572864 | tf_op jit(solution)/shard_map/psum | solution.py:213
  187.4 2.5 copy-start.10
  187.4 2.7 copy-start.19
  194.5 96.0 %reduce-scatter.8.cloned.1.call-start = ((), (), s32[]{:S(2)}) async-start(), calls=%async_computation.7 | async-start | bytes 1966080 | tf_op jit(solution)/shard_map/reduce_scatter | solution.py:394
  229.3 2.1 copy-start.5
  229.3 2.1 copy-start.8
  233.6 2.0 copy-start.13
  245.9 1.8 copy-start.25
  245.9 92.1 %all-reduce.18.cloned.1.call-start = ((), (), s32[]{:S(2)}) async-start(), calls=%async_computation.10 | async-start | bytes 3145728 | tf_op jit(solution)/shard_map/psum | solution.py:213
  247.7 2.1 copy-start.27
  292.7 3.2 copy-start.12
  295.8 3.6 copy-start.14
  295.8 3.6 copy-start.16
  295.8 116.3 %reduce-scatter.12.cloned.1.call-start = ((), (), s32[]{:S(2)}) async-start(), calls=%async_computation.9 | async-start | bytes 3096576
  312.0 165.8 %reduce-scatter.10.cloned.1.call-start = ((), (), s32[]{:S(2)}) async-start(), calls=%async_computation.8 | async-start | bytes 1105920
  338.0 3.1 copy-start.7
  339.4 2.7 copy-start.20
  343.5 2.4 copy-start.9
  (12 other events, 16.1 us)
Sparse Core Ops, SparseCore 0:
  14.8 70.3 all-gather.2
  93.1 35.5 all-gather.4
  140.3 45.0 all-reduce.13
  194.6 34.6 all-reduce.15
  246.0 44.4 reduce-scatter.7
  295.9 42.0 all-reduce.17
  341.5 70.5 reduce-scatter.11
  415.5 62.2 reduce-scatter.9

commit v2 on v1

--- a/solution.py
+++ b/solution.py
@@ -205,8 +205,180 @@
     return lax.all_gather(array, ("shard", "ctx"), axis=0, tiled=True)
 
 
+def greet(partners):
+    barrier = pltpu.get_barrier_semaphore()
+    for partner in partners:
+        pl.semaphore_signal(
+            barrier, inc=1, device_id=partner, device_id_type=pl.DeviceIdType.MESH
+        )
+    pl.semaphore_wait(barrier, len(partners))
+
+
+def send(source, target, send_sem, recv_sem, partner):
+    copy = pltpu.make_async_remote_copy(
+        src_ref=source,
+        dst_ref=target,
+        send_sem=send_sem,
+        recv_sem=recv_sem,
+        device_id=partner,
+        device_id_type=pl.DeviceIdType.MESH,
+    )
+    copy.start()
+    return copy
+
+
+def wide(array):
+    return array.astype(jnp.float32)
+
+
+def sum_kernel(cuts, x_ref, out_ref, near_in, part, far_in, full, near_full, send_sems, recv_sems):
+    me = lax.axis_index("tp")
+    side = lax.rem(me, 2)
+    near = {"tp": me + 1 - 2 * side}
+    far = {"tp": lax.rem(me + 2, 4)}
+    greet((near, far))
+    half = x_ref.shape[0] // 2
+    size = half // cuts
+    mine, other = side * half, (1 - side) * half
+    copies = [[], [], []]
+
+    def rows_at(base, k):
+        return pl.ds(pl.multiple_of(base + k * size, size), size)
+
+    for k in range(cuts):
+        here = pl.ds(k * size, size)
+        copies[0].append(
+            send(
+                x_ref.at[rows_at(other, k)], near_in.at[here],
+                send_sems.at[0, k], recv_sems.at[0, k], near,
+            )
+        )
+    for k in range(cuts):
+        here = pl.ds(k * size, size)
+        copies[0][k].wait_recv()
+        part[here] = (wide(x_ref[rows_at(mine, k)]) + wide(near_in[here])).astype(part.dtype)
+        copies[1].append(
+            send(part.at[here], far_in.at[here], send_sems.at[1, k], recv_sems.at[1, k], far)
+        )
+    for k in range(cuts):
+        here = pl.ds(k * size, size)
+        copies[1][k].wait_recv()
+        total = (wide(part[here]) + wide(far_in[here])).astype(full.dtype)
+        full[here] = total
+        copies[2].append(
+            send(full.at[here], near_full.at[here], send_sems.at[2, k], recv_sems.at[2, k], near)
+        )
+        out_ref[rows_at(mine, k)] = total
+    for k in range(cuts):
+        copies[2][k].wait_recv()
+        out_ref[rows_at(other, k)] = near_full[pl.ds(k * size, size)]
+    for group in copies:
+        for copy in group:
+            copy.wait_send()
+
+
+def sum_tp_direct(array):
+    rows, width = array.shape
+    if lax.axis_size("tp") != 4 or rows % 128 != 0:
+        return lax.psum(array, "tp")
+    cuts = 4
+    vmem = pl.BlockSpec(memory_space=pltpu.VMEM)
+
+    def kernel(*refs):
+        sum_kernel(cuts, *refs)
+
+    return pl.pallas_call(
+        kernel,
+        out_shape=jax.ShapeDtypeStruct(array.shape, array.dtype),
+        in_specs=[vmem],
+        out_specs=vmem,
+        scratch_shapes=[pltpu.VMEM((rows // 2, width), array.dtype)] * 5
+        + [pltpu.SemaphoreType.DMA((3, cuts)), pltpu.SemaphoreType.DMA((3, cuts))],
+        compiler_params=pltpu.CompilerParams(
+            collective_id=0, has_side_effects=True, vmem_limit_bytes=vmem_bytes
+        ),
+    )(array)
+
+
+def scatter_kernel(
+    bounds, count, x_ref, out_ref, shard_in, part, ctx_in, shard_send, shard_recv, ctx_send, ctx_recv
+):
+    mine = lax.axis_index("shard")
+    place = lax.axis_index("ctx")
+    across = {"shard": 1 - mine}
+    targets = [lax.rem(place + hop, count) for hop in range(1, count)]
+    greet([across] + [{"ctx": target} for target in targets])
+    first = []
+    second = []
+    for k, (low_at, size) in enumerate(bounds):
+        lanes = pl.ds(low_at, size)
+        first.append(
+            send(
+                x_ref.at[pl.ds((1 - mine) * count, count), :, lanes], shard_in.at[:, :, lanes],
+                shard_send.at[k], shard_recv.at[k], across,
+            )
+        )
+    for k, (low_at, size) in enumerate(bounds):
+        lanes = pl.ds(low_at, size)
+        first[k].wait_recv()
+        part[:, :, lanes] = (
+            wide(x_ref[pl.ds(mine * count, count), :, lanes]) + wide(shard_in[:, :, lanes])
+        ).astype(part.dtype)
+        second.append(
+            [
+                send(
+                    part.at[target, :, lanes], ctx_in.at[hop, :, lanes],
+                    ctx_send.at[hop, k], ctx_recv.at[hop, k], {"ctx": target},
+                )
+                for hop, target in enumerate(targets)
+            ]
+        )
+    for k, (low_at, size) in enumerate(bounds):
+        lanes = pl.ds(low_at, size)
+        total = wide(part[place, :, lanes])
+        for hop in range(count - 1):
+            second[k][hop].wait_recv()
+            total = total + wide(ctx_in[hop, :, lanes])
+        out_ref[:, lanes] = total
+    for k in range(len(bounds)):
+        first[k].wait_send()
+        for copy in second[k]:
+            copy.wait_send()
+
+
 def scatter_owned(array):
-    return lax.psum_scatter(array, ("shard", "ctx"), scatter_dimension=0, tiled=True)
+    shard_size, count = lax.axis_size("shard"), lax.axis_size("ctx")
+    own, lanes = array.shape[0] // (shard_size * count), array.shape[1]
+    if shard_size != 2:
+        return lax.psum_scatter(
+            array, ("shard", "ctx"), scatter_dimension=0, tiled=True
+        ).astype(jnp.float32)
+    step = 512
+    bounds = [(at, min(step, lanes - at)) for at in range(0, lanes, step)]
+    vmem = pl.BlockSpec(memory_space=pltpu.VMEM)
+
+    def kernel(*refs):
+        scatter_kernel(bounds, count, *refs)
+
+    parts = len(bounds)
+    return pl.pallas_call(
+        kernel,
+        out_shape=jax.ShapeDtypeStruct((own, lanes), jnp.float32),
+        in_specs=[vmem],
+        out_specs=vmem,
+        scratch_shapes=[
+            pltpu.VMEM((count, own, lanes), array.dtype),
+            pltpu.VMEM((count, own, lanes), array.dtype),
+            pltpu.VMEM((count - 1, own, lanes), array.dtype),
+            pltpu.SemaphoreType.DMA((parts,)),
+            pltpu.SemaphoreType.DMA((parts,)),
+            pltpu.SemaphoreType.DMA((count - 1, parts)),
+            pltpu.SemaphoreType.DMA((count - 1, parts)),
+        ],
+        compiler_params=pltpu.CompilerParams(
+            collective_id=1, has_side_effects=True, vmem_limit_bytes=vmem_bytes
+        ),
+    )(array.reshape(shard_size * count, own, lanes))
 
 
 def sum_tp(array):
@@ -329,7 +501,7 @@
         .reshape(rows, mixed_wide)
         .astype(low)
     )
-    branch = sum_tp(outer(mixed_low, proj_full).astype(low)).astype(jnp.float32) + bias_proj
+    branch = sum_tp_direct(outer(mixed_low, proj_full).astype(low)).astype(jnp.float32) + bias_proj
     resid = flat + branch
     norm_second, pull_second = jax.vjp(layer_norm, resid, gain_second, shift_second)
     second_low = norm_second.astype(low)
@@ -341,7 +513,7 @@
     act_grad = jnp.dot(grad_low, down_full, preferred_element_type=jnp.float32)
     (pre_grad,) = pull_gelu(act_grad)
     pre_low = pre_grad.astype(low)
-    norm_two_grad = sum_tp(outer(pre_low, up_full).astype(low)).astype(jnp.float32)
+    norm_two_grad = sum_tp_direct(outer(pre_low, up_full).astype(low)).astype(jnp.float32)
     layer_out = (
         resid + sum_tp(outer(active_low, down_full).astype(low)).astype(jnp.float32) + bias_down
     )
@@ -374,20 +546,6 @@
         ],
         axis=0,
     )
-    second_piece = scatter_owned(
-        pad_lanes(
-            jnp.concatenate(
-                [
-                    inner(second_low, pre_low).astype(low),
-                    inner(grad_low, active_low).astype(low),
-                    inner(branch_low, mixed_low).astype(low),
-                    second_small.T.astype(low),
-                ],
-                axis=1,
-            )
-        )
-    ).astype(jnp.float32)
-
     query_grad, pair_total = attend_back(
         head_size, mine, query_pad, grad_pad, mixed_pad, lse_wide, pairs, seg_q, seg_k
     )
@@ -402,7 +560,7 @@
     qv_bias_grad = jnp.concatenate(
         [summed_bias[:, :head_size], summed_bias[:, 2 * head_size :]], axis=1
     )
-    norm_one_grad = sum_tp(outer(proj_low, qkv_full).astype(low)).astype(jnp.float32)
+    norm_one_grad = sum_tp_direct(outer(proj_low, qkv_full).astype(low)).astype(jnp.float32)
     input_part, gain_one_grad, shift_one_grad = pull_first(norm_one_grad)
     input_grad = resid_grad + input_part
     qv_split = columns_of(
@@ -412,28 +570,30 @@
         [jnp.stack([gain_one_grad, shift_one_grad]), qv_split.transpose(1, 0, 2).reshape(-1, width)],
         axis=0,
     )
-    first_piece = scatter_owned(
-        pad_lanes(
-            jnp.concatenate(
-                [inner(input_low, proj_low).astype(low), first_small.T.astype(low)], axis=1
-            )
-        )
-    ).astype(jnp.float32)
-
-    up_piece = second_piece[:, :hidden]
-    down_piece = second_piece[:, hidden : 2 * hidden].T
+    small_count = second_small.shape[0]
+    pieces = scatter_owned(
+        jnp.concatenate(
+            [
+                inner(second_low, pre_low).astype(low),
+                inner(grad_low, active_low).astype(low),
+                inner(input_low, proj_low).astype(low),
+                inner(branch_low, mixed_low).astype(low),
+                pad_lanes(jnp.concatenate([second_small, first_small], axis=0).T.astype(low)),
+            ],
+            axis=1,
+        )
+    )
+    up_piece = pieces[:, :hidden]
+    down_piece = pieces[:, hidden : 2 * hidden].T
     at = 2 * hidden
-    proj_piece = second_piece[:, at : at + mixed_wide].T.reshape(heads_dev, head_size, own)
+    qkv_piece = pieces[:, at : at + 3 * mixed_wide].reshape(own, heads_dev, 3 * head_size)
+    at += 3 * mixed_wide
+    proj_piece = pieces[:, at : at + mixed_wide].T.reshape(heads_dev, head_size, own)
     at += mixed_wide
-    second_vectors = second_piece[:, at:].T
-    up_bias_piece = second_vectors[4 : 4 + up_bias_split.shape[1]].reshape(-1)[
-        : up_bias.size
-    ].reshape(up_bias.shape)
-    qkv_piece = first_piece[:, : 3 * mixed_wide].reshape(own, heads_dev, 3 * head_size)
-    first_vectors = first_piece[:, 3 * mixed_wide :].T
-    qv_bias_piece = first_vectors[2 : 2 + qv_split.shape[1]].reshape(-1)[: qv_bias.size].reshape(
-        qv_bias.shape
-    )
+    second_vectors = pieces[:, at : at + small_count].T
+    first_vectors = pieces[:, at + small_count : at + small_count + first_small.shape[0]].T
+    up_bias_piece = second_vectors[4:].reshape(-1)[: up_bias.size].reshape(up_bias.shape)
+    qv_bias_piece = first_vectors[2:].reshape(-1)[: qv_bias.size].reshape(qv_bias.shape)
     return (
         layer_out.astype(low).reshape(seq_count, block, width),
         input_grad.reshape(seq_count, block, width),

time: 489 us -> 362 us (0.74)
  waiting for transfers between devices: 367 us -> 145 us
  Pallas kernels: 14.1 us -> 116 us
  other arithmetic: 22.2 us -> 16.5 us
    unnamed x10 -> x4, waiting for transfers between devices: 123 us -> 0.07 us
    psum x3 -> x1, waiting for transfers between devices: 103 us -> 0.01 us  [sum_tp(): return lax.psum(array, 'tp')]
    pallas_call x0 -> x4, Pallas kernels: none -> 102 us  [the longest x1 54 us: scatter_owned(): pl.pallas_call(kernel, out_shape=jax.ShapeDtypeStruct((own, lanes), jnp.f...]
    concatenate x1 -> x3, local copies, waits for them, and re-layouts: 0.04 us -> 6.86 us  [the longest x2 6.81 us: shards(): jnp.concatenate([inner(second_low, pre_low).astype(low), inner(grad_low,...]
    unnamed x65 -> x105, local copies, waits for them, and re-layouts: 19.5 us -> 13.1 us
    pad x3 -> x1, local copies, waits for them, and re-layouts: 5.92 us -> 0.01 us  [pad_lanes(): return jnp.pad(array, [(0, 0)] * (array.ndim - 1) + [(0, extra)])]
  transfers between devices with their start and end apart: 8 -> 4, of which waited for: 8 -> 3; matrix products, arithmetic and copies ran while one was open for 9% -> 12% of each run, Pallas kernels for 0% -> 21%
where the time goes in v2:
time: 362 us; the launch traced here: 360 us
  waiting for transfers between devices  145 us (40%)
  Pallas kernels  116 us (32%)
  local copies, waits for them, and re-layouts  45.5 us (13%)
  matrix products  22.3 us (6%)
  other arithmetic  16.5 us (5%)
  between operations  14.5 us (4%)
    all_gather x1, waiting for transfers between devices, gather_owned(): return lax.all_gather(array, ('shard', 'ctx'), axis=0, tiled=True)  69.9 us
    pallas_call x1, Pallas kernels, scatter_owned(): pl.pallas_call(kernel, out_shape=jax.ShapeDtypeStruct((own, lanes), jnp.f...  54 us
    pallas_call x3, Pallas kernels, sum_tp_direct(): pl.pallas_call(kernel, out_shape=jax.ShapeDtypeStruct(array.shape, array....  47.9 us
    reduce_scatter x1, waiting for transfers between devices, shards(): lax.psum_scatter(pair_total, 'ctx', scatter_dimension=0, tiled=True)  41.5 us
    all_gather x1, waiting for transfers between devices, shards(): lax.all_gather(pair_own.reshape(rows, 2 * mixed_wide), 'ctx', axis=0, til...  34 us
    unnamed x105, local copies, waits for them, and re-layouts  13.1 us
    pallas_call x1, Pallas kernels, attend_back(): pl.pallas_call(backward_kernel, grid_spec=pltpu.PrefetchScalarGridSpec(nu...  8.57 us
    dot_general x4, matrix products, inner(): lax.dot_general(left, right, (((0,), (0,)), ((), ())), preferred_element_...  8.25 us
  transfers between devices with their start and end apart: 4, of which 3 were waited for; matrix products, arithmetic and copies ran while one was open for 12% of the time, Pallas kernels for 21%

profile of v2, /device:TPU:0, one launch (start us, length us, event | category | flops | bytes accessed | tf_op | source)
XLA Modules:
  0.0 360.5 jit_solution(9718835288496807952)
XLA Ops:
  12.8 1.9 concatenate.34
  15.3 69.9 %all-gather.3.cloned.1.call-done = bf16[768,2432]{1,0:T(8,128)(2,1)} async-done(((bf16[96,2432]{1,0:T(8,128)(2,1)}), bf16[768,2432]{1,0:T(8,128)(2,1)}) %all-gather.3.cloned.1.call-update) | async-done | bytes 3735568 | tf_op jit(solution)/shard_map/all_gather | solution.py:205
  90.9 2.0 fusion.45
  95.7 34.0 %all-gather.5.cloned.1.call-done.pair_ref = bf16[2048,384]{1,0:T(8,128)(2,1)} async-done(((bf16[512,384]{1,0:T(8,128)(2,1)}), bf16[2048,384]{1,0:T(8,128)(2,1)}) %all-gather.5.cloned.1.call-update) | async-done | bytes 1572880 | tf_op jit(solution)/shard_map/all_gather | solution.py:497
  131.2 5.4 %shard_map.254 = (f32[512,384]{1,0:T(8,128)S(1)}, f32[512,384]{1,0:T(8,128)S(1)}) custom-call(s32[1]{0:T(128)} %bitcast.1.mine_ref, bf16[512,384]{1,0:T(8,128)(2,1)S(1)} %copy.75.query_ref, bf16[2048,384]{1,0:T(8,128)(2,1)S(1)} %copy-done.4, s32[512,128]{1,0:T(8,128)S(1)} %broadcast_in_dim.10.seg_q_ref, s32[4,1,512]{2,1,0:T(1,128)S(1)} %reshape.282.seg_k_ref), custom_call_target="tpu_custom_call" | custom-call | flops 1610612736 | bytes 3145728 | tf_op jit(solution)/shard_map/pallas_call | solution.py:125
  136.9 1.7 convolution_convert_fusion.6.refs_0_
  138.6 13.9 %shard_map.255 = bf16[512,768]{1,0:T(8,128)(2,1)S(1)} custom-call(bf16[512,768]{1,0:T(8,128)(2,1)S(1)} %convolution_convert_fusion.6.refs_0_), custom_call_target="tpu_custom_call" | custom-call | tf_op jit(solution)/shard_map/pallas_call | solution.py:290
  154.5 2.4 fusion.68
  158.6 13.9 %shard_map.256 = bf16[512,768]{1,0:T(8,128)(2,1)S(1)} custom-call(bf16[512,768]{1,0:T(8,128)(2,1)S(1)} %convolution_convert_fusion.3.refs_0_), custom_call_target="tpu_custom_call" | custom-call | tf_op jit(solution)/shard_map/pallas_call | solution.py:290
  173.1 1.6 fusion.10
  183.2 8.6 %shard_map.257 = (f32[512,384]{1,0:T(8,128)S(1)}, bf16[2048,384]{1,0:T(8,128)(2,1)}) custom-call(s32[1]{0:T(128)} %bitcast.1.mine_ref, bf16[512,384]{1,0:T(8,128)(2,1)S(1)} %copy.75.query_ref, bf16[512,384]{1,0:T(8,128)(2,1)S(1)} %copy-done.1, f32[512,384]{1,0:T(8,128)S(1)} %get-tuple-element.18.mixed_ref, f32[512,384]{1,0:T(8,128)S(1)} %copy-done.7, ...), custom_call_target="tpu_custom_call" | custom-call | flops 4026531840 | bytes 4718592 | tf_op jit(solution)/shard_map/pallas_call | solution.py:160
  196.6 3.4 fusion.27
  200.0 2.0 fusion.30
  202.0 3.2 convolution_convert_fusion.4
  205.2 41.5 %reduce-scatter.2.cloned.1.call-done = bf16[512,384]{1,0:T(8,128)(2,1)} async-done(((bf16[2048,384]{1,0:T(8,128)(2,1)}), bf16[512,384]{1,0:T(8,128)(2,1)}) %reduce-scatter.2.cloned.1.call-update) | async-done | bytes 393232 | tf_op jit(solution)/shard_map/reduce_scatter | solution.py:552
  248.2 2.3 convolution_convert_fusion.5.refs_0_
  250.4 20.2 %shard_map.258 = bf16[512,768]{1,0:T(8,128)(2,1)S(1)} custom-call(bf16[512,768]{1,0:T(8,128)(2,1)S(1)} %convolution_convert_fusion.5.refs_0_), custom_call_target="tpu_custom_call" | custom-call | tf_op jit(solution)/shard_map/pallas_call | solution.py:290
  272.9 1.8 fusion.28
  276.9 6.1 %copy.84 = bf16[768,2432]{1,0:T(8,128)(2,1)} copy(bf16[768,2432]{0,1:T(8,128)(2,1)} %pad_dynamic-update-slice_fusion) | data formatting | bytes 7471104 | tf_op jit(solution)/shard_map/concatenate | solution.py:575
  283.0 2.1 copy-done
  285.1 54.0 %shard_map.259 = f32[96,2432]{1,0:T(8,128)S(1)} custom-call(bf16[8,96,2432]{2,1,0:T(8,128)(2,1)S(1)} %bitcast.147), custom_call_target="tpu_custom_call" | custom-call | tf_op jit(solution)/shard_map/pallas_call | solution.py:364
  342.4 1.8 copy.87
  345.5 1.6 copy.86
  350.0 4.0 %add_bitcast_fusion = (f32[1,512,768]{2,1,0:T(8,128)}, bf16[1,512,768]{2,1,0:T(8,128)(2,1)}) fusion(bf16[1,512,768]{2,1,0:T(8,128)(2,1)} %param.15, bf16[512,768]{1,0:T(8,128)(2,1)S(1)} %shard_map.258, bf16[1,512,768]{2,1,0:T(8,128)(2,1)} %param.29, f32[512]{0:T(512)S(1)} %negate_multiply_fusion, f32[512]{0:T(512)} %copy-done.30, f32[512]{0:T(512)} %copy-done.31, ...), kind=kLoop, calls=%fused_computation.42 | loop fusion | flops 10616832 | bytes 7106560 | tf_op jit(solution)/shard_map/reshape | solution.py:599
  (211 shorter events, 46.9 us)
Async XLA Ops:
  7.2 7.6 %copy-start.8 = (bf16[1,512,768]{2,1,0:T(8,128)(2,1)S(1)}, bf16[1,512,768]{2,1,0:T(8,128)(2,1)}, u32[]{:S(2)}) copy-start(bf16[1,512,768]{2,1,0:T(8,128)(2,1)} %param.15) | copy-start | bytes 2359300
  7.2 78.0 %all-gather.3.cloned.1.call-start = ((), (), s32[]{:S(2)}) async-start(), calls=%async_computation.1 | async-start | bytes 4202496 | tf_op jit(solution)/shard_map/all_gather | solution.py:205
  14.7 115.0 %all-gather.5.cloned.1.call-start = ((), (), s32[]{:S(2)}) async-start(), calls=%async_computation.2 | async-start | bytes 1966080 | tf_op jit(solution)/shard_map/all_gather | solution.py:497
  14.9 75.9 %copy-start.25 = (f32[512]{0:T(512)}, f32[512]{0:T(512)S(1)}, u32[]{:S(2)}) copy-start(f32[512]{0:T(512)S(1)} %broadcast_multiply_fusion.1) | copy-start | bytes 6148
  15.3 72.4 %copy-start.34 = (f32[512]{0:T(512)}, f32[512]{0:T(512)S(1)}, u32[]{:S(2)}) copy-start(f32[512]{0:T(512)S(1)} %fusion.12) | copy-start | bytes 6148
  15.3 75.5 %copy-start.31 = (f32[512]{0:T(512)}, f32[512]{0:T(512)S(1)}, u32[]{:S(2)}) copy-start(f32[512]{0:T(512)S(1)} %fusion.53) | copy-start | bytes 6148
  94.0 152.8 %reduce-scatter.2.cloned.1.call-start = ((), (), s32[]{:S(2)}) async-start(), calls=%async_computation.4 | async-start | bytes 1966080 | tf_op jit(solution)/shard_map/reduce_scatter | solution.py:552
  94.1 35.5 %copy-start.38 = (s32[1,512]{1,0:T(1,128)S(1)}, s32[1,512]{1,0:T(1,128)}, u32[]{:S(2)}) copy-start(s32[1,512]{1,0:T(1,128)} %param.16) | copy-start | bytes 6148
  131.2 5.4 %copy-start.2 = (s32[512,128]{1,0:T(8,128)}, s32[512,128]{1,0:T(8,128)S(1)}, u32[]{:S(2)}) copy-start(s32[512,128]{1,0:T(8,128)S(1)} %broadcast_in_dim.10.seg_q_ref) | copy-start | bytes 786436
  136.9 16.0 %copy-start.15 = (bf16[512,3,64]{0,2,1:T(8,128)(2,1)}, bf16[512,3,64]{0,2,1:T(8,128)(2,1)S(1)}, u32[]{:S(2)}) copy-start(bf16[512,3,64]{0,2,1:T(8,128)(2,1)S(1)} %slice.179) | copy-start | bytes 589828
  138.6 14.7 %copy-start.17 = (bf16[768,2432]{1,0:T(8,128)(2,1)S(1)}, bf16[768,2432]{1,0:T(8,128)(2,1)}, u32[]{:S(2)}) copy-start(bf16[768,2432]{1,0:T(8,128)(2,1)} %all-gather.3.cloned.1.call-done) | copy-start | bytes 11206660
  152.9 21.8 %copy-start.20 = (f32[512]{0:T(512)}, f32[512]{0:T(512)S(1)}, u32[]{:S(2)}) copy-start(f32[512]{0:T(512)S(1)} %broadcast_multiply_fusion) | copy-start | bytes 6148
  153.4 21.4 %copy-start.28 = (f32[512]{0:T(512)}, f32[512]{0:T(512)S(1)}, u32[]{:S(2)}) copy-start(f32[512]{0:T(512)S(1)} %fusion.54) | copy-start | bytes 6148
  191.9 4.6 %copy-start.9 = (bf16[1,512,768]{2,1,0:T(8,128)(2,1)S(1)}, bf16[1,512,768]{2,1,0:T(8,128)(2,1)}, u32[]{:S(2)}) copy-start(bf16[1,512,768]{2,1,0:T(8,128)(2,1)} %param.15) | copy-start | bytes 2359300
  191.9 4.6 %copy-start.21 = (f32[512]{0:T(512)S(1)}, f32[512]{0:T(512)}, u32[]{:S(2)}) copy-start(f32[512]{0:T(512)} %copy-done.20) | copy-start | bytes 6148
  191.9 4.6 %copy-start.29 = (f32[512]{0:T(512)S(1)}, f32[512]{0:T(512)}, u32[]{:S(2)}) copy-start(f32[512]{0:T(512)} %copy-done.28) | copy-start | bytes 6148
  191.9 4.6 %copy-start.45 = (f32[768]{0:T(1024)S(1)}, f32[768]{0:T(1024)}, u32[]{:S(2)}) copy-start(f32[768]{0:T(1024)} %get-tuple-element.69) | copy-start | bytes 9220
  191.9 158.1 %all-reduce.10.cloned.1.call-start = ((), (), s32[]{:S(2)}) async-start(), calls=%async_computation.3 | async-start | bytes 1572864 | tf_op jit(solution)/shard_map/psum | solution.py:385
  248.1 22.5 %copy-start.18 = (bf16[512,3,192]{0,2,1:T(8,128)(2,1)}, bf16[512,3,192]{0,2,1:T(8,128)(2,1)S(1)}, u32[]{:S(2)}) copy-start(bf16[512,3,192]{0,2,1:T(8,128)(2,1)S(1)} %get-tuple-element.89) | copy-start | bytes 1769476
  248.1 22.5 %copy-start.10 = (bf16[1,512,768]{2,1,0:T(8,128)(2,1)S(1)}, bf16[1,512,768]{2,1,0:T(8,128)(2,1)}, u32[]{:S(2)}) copy-start(bf16[1,512,768]{2,1,0:T(8,128)(2,1)} %param.15) | copy-start | bytes 2359300
  248.1 22.5 %copy-start.24 = (f32[768]{0:T(1024)S(1)}, f32[768]{0:T(1024)}, u32[]{:S(2)}) copy-start(f32[768]{0:T(1024)} %copy-done.23) | copy-start | bytes 9220
  248.2 22.5 %copy-start.26 = (f32[512]{0:T(512)S(1)}, f32[512]{0:T(512)}, u32[]{:S(2)}) copy-start(f32[512]{0:T(512)} %copy-done.25) | copy-start | bytes 6148
  339.2 10.8 %copy-start.22 = (f32[512]{0:T(512)S(1)}, f32[512]{0:T(512)}, u32[]{:S(2)}) copy-start(f32[512]{0:T(512)} %copy-done.20) | copy-start | bytes 6148
  342.4 7.6 %copy-start.36 = (f32[768]{0:T(1024)S(1)}, f32[768]{0:T(1024)}, u32[]{:S(2)}) copy-start(f32[768]{0:T(1024)} %get-tuple-element.68) | copy-start | bytes 9220
  (31 other events, 63.7 us)
Sparse Core Ops, SparseCore 0:
  14.8 70.3 all-gather.2
  94.1 35.5 all-gather.4
  191.9 54.7 reduce-scatter.1
  249.6 37.1 all-reduce.9

commit v3 on v2

--- a/solution.py
+++ b/solution.py
@@ -201,10 +201,6 @@
     return jnp.pad(array, [(0, 0)] * (array.ndim - 1) + [(0, extra)])
 
 
-def gather_owned(array):
-    return lax.all_gather(array, ("shard", "ctx"), axis=0, tiled=True)
-
-
 def greet(partners):
     barrier = pltpu.get_barrier_semaphore()
     for partner in partners:
@@ -229,6 +225,85 @@
 
 def wide(array):
     return array.astype(jnp.float32)
+
+
+def gather_kernel(
+    bounds, count, x_ref, out_ref, shard_send, shard_recv, ctx_send, ctx_recv
+):
+    mine = lax.axis_index("shard")
+    place = lax.axis_index("ctx")
+    across = {"shard": 1 - mine}
+    targets = [lax.rem(place + hop, count) for hop in range(1, count)]
+    greet([across] + [{"ctx": target} for target in targets])
+    here = mine * count + place
+    first = []
+    second = []
+    for k, (low_at, size) in enumerate(bounds):
+        lanes = pl.ds(low_at, size)
+        first.append(
+            [
+                send(
+                    x_ref.at[:, lanes], out_ref.at[here, :, lanes],
+                    ctx_send.at[hop, k], ctx_recv.at[hop, k], {"ctx": target},
+                )
+                for hop, target in enumerate(targets)
+            ]
+        )
+        second.append(
+            [
+                send(
+                    x_ref.at[:, lanes], out_ref.at[here, :, lanes],
+                    shard_send.at[0, k], shard_recv.at[0, k], across,
+                )
+            ]
+        )
+    out_ref[here] = x_ref[...]
+    for k, (low_at, size) in enumerate(bounds):
+        lanes = pl.ds(low_at, size)
+        for hop in range(1, count):
+            arrived = mine * count + lax.rem(place - hop + count, count)
+            first[k][hop - 1].wait_recv()
+            second[k].append(
+                send(
+                    out_ref.at[arrived, :, lanes], out_ref.at[arrived, :, lanes],
+                    shard_send.at[hop, k], shard_recv.at[hop, k], across,
+                )
+            )
+    for k in range(len(bounds)):
+        for copy in second[k]:
+            copy.wait()
+        for copy in first[k]:
+            copy.wait_send()
+
+
+def gather_owned(array):
+    shard_size, count = lax.axis_size("shard"), lax.axis_size("ctx")
+    own, lanes = array.shape
+    if shard_size != 2:
+        return lax.all_gather(array, ("shard", "ctx"), axis=0, tiled=True)
+    step = 896
+    bounds = [(at, min(step, lanes - at)) for at in range(0, lanes, step)]
+    vmem = pl.BlockSpec(memory_space=pltpu.VMEM)
+
+    def kernel(*refs):
+        gather_kernel(bounds, count, *refs)
+
+    parts = len(bounds)
+    return pl.pallas_call(
+        kernel,
+        out_shape=jax.ShapeDtypeStruct((shard_size * count, own, lanes), array.dtype),
+        in_specs=[vmem],
+        out_specs=vmem,
+        scratch_shapes=[
+            pltpu.SemaphoreType.DMA((count, parts)),
+            pltpu.SemaphoreType.DMA((count, parts)),
+            pltpu.SemaphoreType.DMA((count - 1, parts)),
+            pltpu.SemaphoreType.DMA((count - 1, parts)),
+        ],
+        compiler_params=pltpu.CompilerParams(
+            collective_id=2, has_side_effects=True, vmem_limit_bytes=vmem_bytes
+        ),
+    )(array).reshape(shard_size * count * own, lanes)
 
 
 def sum_kernel(cuts, x_ref, out_ref, near_in, part, far_in, full, near_full, send_sems, recv_sems):

time: 362 us -> 346 us (0.956)
  waiting for transfers between devices: 145 us -> 79.1 us
  Pallas kernels: 116 us -> 171 us
    all_gather x1 -> x0, waiting for transfers between devices: 69.9 us -> none  [gather_owned(): return lax.all_gather(array, ('shard', 'ctx'), axis=0, tiled=True)]
    pallas_call x0 -> x1, Pallas kernels: none -> 55.2 us  [gather_owned(): pl.pallas_call(kernel, out_shape=jax.ShapeDtypeStruct((shard_size * count...]
    unnamed x105 -> x109, local copies, waits for them, and re-layouts: 13.1 us -> 14.9 us
  transfers between devices with their start and end apart: 4 -> 3, of which waited for: 3 -> 2; matrix products, arithmetic and copies ran while one was open for 12% -> 12% of each run, Pallas kernels for 21% -> 21%
where the time goes in v3:
time: 346 us; the launch traced here: 345 us
  Pallas kernels  171 us (49%)
  waiting for transfers between devices  79.1 us (23%)
  local copies, waits for them, and re-layouts  43.6 us (13%)
  matrix products  21.1 us (6%)
  other arithmetic  15.6 us (5%)
  between operations  14.5 us (4%)
    pallas_call x1, Pallas kernels, gather_owned(): pl.pallas_call(kernel, out_shape=jax.ShapeDtypeStruct((shard_size * count...  55.2 us
    pallas_call x1, Pallas kernels, scatter_owned(): pl.pallas_call(kernel, out_shape=jax.ShapeDtypeStruct((own, lanes), jnp.f...  54 us
    pallas_call x3, Pallas kernels, sum_tp_direct(): pl.pallas_call(kernel, out_shape=jax.ShapeDtypeStruct(array.shape, array....  47.9 us
    reduce_scatter x1, waiting for transfers between devices, shards(): lax.psum_scatter(pair_total, 'ctx', scatter_dimension=0, tiled=True)  41.5 us
    all_gather x1, waiting for transfers between devices, shards(): lax.all_gather(pair_own.reshape(rows, 2 * mixed_wide), 'ctx', axis=0, til...  37.5 us
    unnamed x109, local copies, waits for them, and re-layouts  14.9 us
    pallas_call x1, Pallas kernels, attend_back(): pl.pallas_call(backward_kernel, grid_spec=pltpu.PrefetchScalarGridSpec(nu...  8.57 us
    dot_general x4, matrix products, inner(): lax.dot_general(left, right, (((0,), (0,)), ((), ())), preferred_element_...  8.25 us
  transfers between devices with their start and end apart: 3, of which 2 were waited for; matrix products, arithmetic and copies ran while one was open for 12% of the time, Pallas kernels for 21%

profile of v3, /device:TPU:0, one launch (start us, length us, event | category | flops | bytes accessed | tf_op | source)
XLA Modules:
  0.0 345.3 jit_solution(10942180175664633712)
XLA Ops:
  13.8 55.2 %shard_map.254 = bf16[8,96,2432]{2,1,0:T(8,128)(2,1)S(1)} custom-call(bf16[96,2432]{1,0:T(8,128)(2,1)S(1)} %concatenate.34.refs_0_), custom_call_target="tpu_custom_call" | custom-call | tf_op jit(solution)/shard_map/pallas_call | solution.py:292
  69.1 1.7 copy-done.1
  77.5 37.5 %all-gather.2.cloned.1.call-done.pair_ref = bf16[2048,384]{1,0:T(8,128)(2,1)} async-done(((bf16[512,384]{1,0:T(8,128)(2,1)}), bf16[2048,384]{1,0:T(8,128)(2,1)}) %all-gather.2.cloned.1.call-update) | async-done | bytes 1572880 | tf_op jit(solution)/shard_map/all_gather | solution.py:572
  116.6 5.4 %shard_map.255 = (f32[512,384]{1,0:T(8,128)S(1)}, f32[512,384]{1,0:T(8,128)S(1)}) custom-call(s32[1]{0:T(128)} %bitcast.1.mine_ref, bf16[512,384]{1,0:T(8,128)(2,1)S(1)} %copy.114.query_ref, bf16[2048,384]{1,0:T(8,128)(2,1)S(1)} %copy-done.6, s32[512,128]{1,0:T(8,128)S(1)} %broadcast_in_dim.10.seg_q_ref, s32[4,1,512]{2,1,0:T(1,128)S(1)} %reshape.286.seg_k_ref), custom_call_target="tpu_custom_call" | custom-call | flops 1610612736 | bytes 3145728 | tf_op jit(solution)/shard_map/pallas_call | solution.py:125
  122.3 1.7 convolution_convert_fusion.6.refs_0_
  124.0 13.9 %shard_map.256 = bf16[512,768]{1,0:T(8,128)(2,1)S(1)} custom-call(bf16[512,768]{1,0:T(8,128)(2,1)S(1)} %convolution_convert_fusion.6.refs_0_), custom_call_target="tpu_custom_call" | custom-call | tf_op jit(solution)/shard_map/pallas_call | solution.py:365
  139.9 2.4 fusion.68
  144.0 13.9 %shard_map.257 = bf16[512,768]{1,0:T(8,128)(2,1)S(1)} custom-call(bf16[512,768]{1,0:T(8,128)(2,1)S(1)} %convolution_convert_fusion.3.refs_0_), custom_call_target="tpu_custom_call" | custom-call | tf_op jit(solution)/shard_map/pallas_call | solution.py:365
  158.5 1.6 fusion.10
  160.1 1.6 fusion.64
  168.0 8.6 %shard_map.258 = (f32[512,384]{1,0:T(8,128)S(1)}, bf16[2048,384]{1,0:T(8,128)(2,1)}) custom-call(s32[1]{0:T(128)} %bitcast.1.mine_ref, bf16[512,384]{1,0:T(8,128)(2,1)S(1)} %copy.114.query_ref, bf16[512,384]{1,0:T(8,128)(2,1)S(1)} %copy-done.3, f32[512,384]{1,0:T(8,128)S(1)} %get-tuple-element.18.mixed_ref, f32[512,384]{1,0:T(8,128)S(1)} %copy-done.9, ...), custom_call_target="tpu_custom_call" | custom-call | flops 4026531840 | bytes 4718592 | tf_op jit(solution)/shard_map/pallas_call | solution.py:160
  181.4 3.4 fusion.27
  184.8 2.0 fusion.30
  186.8 3.2 convolution_convert_fusion.4
  190.0 41.5 %reduce-scatter.2.cloned.1.call-done = bf16[512,384]{1,0:T(8,128)(2,1)} async-done(((bf16[2048,384]{1,0:T(8,128)(2,1)}), bf16[512,384]{1,0:T(8,128)(2,1)}) %reduce-scatter.2.cloned.1.call-update) | async-done | bytes 393232 | tf_op jit(solution)/shard_map/reduce_scatter | solution.py:627
  233.0 2.3 convolution_convert_fusion.5.refs_0_
  235.3 20.2 %shard_map.259 = bf16[512,768]{1,0:T(8,128)(2,1)S(1)} custom-call(bf16[512,768]{1,0:T(8,128)(2,1)S(1)} %convolution_convert_fusion.5.refs_0_), custom_call_target="tpu_custom_call" | custom-call | tf_op jit(solution)/shard_map/pallas_call | solution.py:365
  257.8 1.8 fusion.28
  261.7 6.1 %copy.123 = bf16[768,2432]{1,0:T(8,128)(2,1)} copy(bf16[768,2432]{0,1:T(8,128)(2,1)} %pad_dynamic-update-slice_fusion) | data formatting | bytes 7471104 | tf_op jit(solution)/shard_map/concatenate | solution.py:650
  267.9 2.1 copy-done
  269.9 54.0 %shard_map.260 = f32[96,2432]{1,0:T(8,128)S(1)} custom-call(bf16[8,96,2432]{2,1,0:T(8,128)(2,1)S(1)} %bitcast.149), custom_call_target="tpu_custom_call" | custom-call | tf_op jit(solution)/shard_map/pallas_call | solution.py:439
  327.2 1.8 copy.126
  330.4 1.6 copy.125
  334.8 4.0 %add_bitcast_fusion = (f32[1,512,768]{2,1,0:T(8,128)}, bf16[1,512,768]{2,1,0:T(8,128)(2,1)}) fusion(bf16[1,512,768]{2,1,0:T(8,128)(2,1)} %param.15, bf16[512,768]{1,0:T(8,128)(2,1)S(1)} %shard_map.259, bf16[1,512,768]{2,1,0:T(8,128)(2,1)} %param.29, f32[512]{0:T(512)S(1)} %negate_multiply_fusion, f32[512]{0:T(512)} %copy-done.32, f32[512]{0:T(512)} %copy-done.33, ...), kind=kLoop, calls=%fused_computation.42 | loop fusion | flops 10616832 | bytes 7106560 | tf_op jit(solution)/shard_map/reshape | solution.py:674
  (218 shorter events, 43.4 us)
Async XLA Ops:
  7.2 107.9 %all-gather.2.cloned.1.call-start = ((), (), s32[]{:S(2)}) async-start(), calls=%async_computation.1 | async-start | bytes 1966080 | tf_op jit(solution)/shard_map/all_gather | solution.py:572
  76.1 39.0 %copy-start.40 = (s32[1,512]{1,0:T(1,128)S(1)}, s32[1,512]{1,0:T(1,128)}, u32[]{:S(2)}) copy-start(s32[1,512]{1,0:T(1,128)} %param.16) | copy-start | bytes 6148
  76.1 155.5 %reduce-scatter.2.cloned.1.call-start = ((), (), s32[]{:S(2)}) async-start(), calls=%async_computation.3 | async-start | bytes 1966080 | tf_op jit(solution)/shard_map/reduce_scatter | solution.py:627
  116.6 5.4 %copy-start.4 = (s32[512,128]{1,0:T(8,128)}, s32[512,128]{1,0:T(8,128)S(1)}, u32[]{:S(2)}) copy-start(s32[512,128]{1,0:T(8,128)S(1)} %broadcast_in_dim.10.seg_q_ref) | copy-start | bytes 786436
  122.3 16.0 %copy-start.17 = (bf16[512,3,64]{0,2,1:T(8,128)(2,1)}, bf16[512,3,64]{0,2,1:T(8,128)(2,1)S(1)}, u32[]{:S(2)}) copy-start(bf16[512,3,64]{0,2,1:T(8,128)(2,1)S(1)} %slice.179) | copy-start | bytes 589828
  124.0 14.7 %copy-start.2 = (bf16[8,96,2432]{2,1,0:T(8,128)(2,1)S(1)}, bf16[8,96,2432]{2,1,0:T(8,128)(2,1)}, u32[]{:S(2)}) copy-start(bf16[8,96,2432]{2,1,0:T(8,128)(2,1)} %copy-done.1) | copy-start | bytes 11206660
  138.3 21.8 %copy-start.22 = (f32[512]{0:T(512)}, f32[512]{0:T(512)S(1)}, u32[]{:S(2)}) copy-start(f32[512]{0:T(512)S(1)} %broadcast_multiply_fusion) | copy-start | bytes 6148
  138.8 21.3 %copy-start.30 = (f32[512]{0:T(512)}, f32[512]{0:T(512)S(1)}, u32[]{:S(2)}) copy-start(f32[512]{0:T(512)S(1)} %fusion.54) | copy-start | bytes 6148
  176.6 3.4 copy-start.42
  176.7 3.4 copy-start.41
  176.7 3.4 copy-start.49
  176.7 4.6 %copy-start.11 = (bf16[1,512,768]{2,1,0:T(8,128)(2,1)S(1)}, bf16[1,512,768]{2,1,0:T(8,128)(2,1)}, u32[]{:S(2)}) copy-start(bf16[1,512,768]{2,1,0:T(8,128)(2,1)} %param.15) | copy-start | bytes 2359300
  176.7 4.6 %copy-start.23 = (f32[512]{0:T(512)S(1)}, f32[512]{0:T(512)}, u32[]{:S(2)}) copy-start(f32[512]{0:T(512)} %copy-done.22) | copy-start | bytes 6148
  176.7 4.6 %copy-start.31 = (f32[512]{0:T(512)S(1)}, f32[512]{0:T(512)}, u32[]{:S(2)}) copy-start(f32[512]{0:T(512)} %copy-done.30) | copy-start | bytes 6148
  176.7 4.6 %copy-start.48 = (f32[768]{0:T(1024)S(1)}, f32[768]{0:T(1024)}, u32[]{:S(2)}) copy-start(f32[768]{0:T(1024)} %get-tuple-element.83) | copy-start | bytes 9220
  176.7 158.1 %all-reduce.10.cloned.1.call-start = ((), (), s32[]{:S(2)}) async-start(), calls=%async_computation.2 | async-start | bytes 1572864 | tf_op jit(solution)/shard_map/psum | solution.py:460
  181.3 3.4 copy-start.14
  181.4 3.4 copy-start.52
  233.0 22.5 %copy-start.19 = (bf16[512,3,192]{0,2,1:T(8,128)(2,1)}, bf16[512,3,192]{0,2,1:T(8,128)(2,1)S(1)}, u32[]{:S(2)}) copy-start(bf16[512,3,192]{0,2,1:T(8,128)(2,1)S(1)} %get-tuple-element.103) | copy-start | bytes 1769476
  233.0 22.5 %copy-start.12 = (bf16[1,512,768]{2,1,0:T(8,128)(2,1)S(1)}, bf16[1,512,768]{2,1,0:T(8,128)(2,1)}, u32[]{:S(2)}) copy-start(bf16[1,512,768]{2,1,0:T(8,128)(2,1)} %param.15) | copy-start | bytes 2359300
  233.0 22.5 %copy-start.26 = (f32[768]{0:T(1024)S(1)}, f32[768]{0:T(1024)}, u32[]{:S(2)}) copy-start(f32[768]{0:T(1024)} %copy-done.25) | copy-start | bytes 9220
  233.0 22.5 %copy-start.28 = (f32[512]{0:T(512)S(1)}, f32[512]{0:T(512)}, u32[]{:S(2)}) copy-start(f32[512]{0:T(512)} %copy-done.27) | copy-start | bytes 6148
  324.1 10.8 %copy-start.24 = (f32[512]{0:T(512)S(1)}, f32[512]{0:T(512)}, u32[]{:S(2)}) copy-start(f32[512]{0:T(512)} %copy-done.22) | copy-start | bytes 6148
  327.2 7.6 %copy-start.38 = (f32[768]{0:T(1024)S(1)}, f32[768]{0:T(1024)}, u32[]{:S(2)}) copy-start(f32[768]{0:T(1024)} %get-tuple-element.82) | copy-start | bytes 9220
  (33 other events, 55.3 us)
Sparse Core Ops, SparseCore 0:
  76.2 38.8 all-gather.1
  176.8 54.7 reduce-scatter.1
  234.5 37.0 all-reduce.9
